TPU v7x, 128 devices: a whole 4x4x4 slice. The times are simulated.
128 devices in a mesh: row: 32 (over z, y, core), ch: 4 (over x).
Axes of the slice: x: 4, y: 4, z: 4, core: 2. Of those that a mesh axis runs over, the one named last changes fastest.
Arguments:
- pair_act: bfloat16 [512, 512, 128], P('row', 'ch'), may hold values from -6 to 6
- valid_count: int32 [1], replicated, may hold values from 257 to 512
- edge_proj: bfloat16 [128, 256], replicated, may hold values from -0.5 to 0.5
- edge_gate: bfloat16 [128, 256], replicated, may hold values from -0.5 to 0.5
- tri_gate: bfloat16 [128, 128], replicated, may hold values from -0.5 to 0.5
- tri_out: bfloat16 [128, 128], replicated, may hold values from -0.5 to 0.5
- attn_proj: bfloat16 [128, 512], replicated, may hold values from -0.5 to 0.5
- bias_proj: bfloat16 [128, 4], replicated, may hold values from -24 to 24, as said below
- attn_out: bfloat16 [128, 128], replicated, may hold values from -0.5 to 0.5
Outputs:
- pair_out: bfloat16 [512, 512, 128], P('row', 'ch')
Inputs may be any that keep to these rules, and one draw needn't show every extreme that they name: `bias_proj`: biases' projection; its columns differ in scale.
All inputs are finite; a program needn't handle non-finite values.
Results may differ from a plain program's by a relative error of at most 0.038.
Values may be sent and summed in bfloat16 or wider, within the bound.
A program may use at most 128 MiB of HBM per device.

v0:
```python
import jax
import jax.numpy as jnp
from jax import lax
from jax.sharding import PartitionSpec as P

EPS = 1e-05


def layer_norm(values):
    centre = values - jnp.mean(values, axis=-1, keepdims=True)
    spread = jnp.mean(centre * centre, axis=-1, keepdims=True)
    return centre * lax.rsqrt(spread + EPS)


def local(
    pair_act, valid_count, edge_proj, edge_gate, tri_gate, tri_out, attn_proj, bias_proj, attn_out
):
    row_count = pair_act.shape[0]
    col_count = pair_act.shape[1]
    channels = pair_act.shape[2]
    head_count = bias_proj.shape[1]
    head_size = channels // head_count
    row_devices = lax.axis_size("row")
    col_devices = lax.axis_size("ch")
    tokens = row_count * row_devices
    row_offset = lax.axis_index("row") * row_count
    col_offset = lax.axis_index("ch") * col_count
    length = valid_count[0]
    row_valid = (row_offset + jnp.arange(row_count) < length).astype(jnp.float32)
    col_valid = (col_offset + jnp.arange(col_count) < length).astype(jnp.float32)
    key_valid = (jnp.arange(tokens) < length).astype(jnp.float32)
    pair_valid = row_valid[:, None] * col_valid[None, :]
    source = pair_act.astype(jnp.float32)
    normed = layer_norm(source).astype(jnp.bfloat16)
    projected = jnp.dot(normed, edge_proj, preferred_element_type=jnp.float32)
    gating = jnp.dot(normed, edge_gate, preferred_element_type=jnp.float32)
    edges = (jax.nn.sigmoid(gating) * projected * pair_valid[:, :, None]).astype(jnp.bfloat16)
    left_edges = edges[:, :, :channels]
    right_edges = edges[:, :, channels:]
    partial_sums = jnp.einsum(
        "ikc,jkc->ijc",
        left_edges,
        lax.all_gather(right_edges, "row", axis=0, tiled=True),
        preferred_element_type=jnp.float32,
    )
    triangle = lax.psum_scatter(partial_sums, "ch", scatter_dimension=1, tiled=True)
    tri_normed = layer_norm(triangle).astype(jnp.bfloat16)
    update = jax.nn.sigmoid(
        jnp.dot(normed, tri_gate, preferred_element_type=jnp.float32)
    ) * jnp.dot(tri_normed, tri_out, preferred_element_type=jnp.float32)
    updated = (source + update).astype(jnp.bfloat16)
    attn_normed = layer_norm(updated.astype(jnp.float32)).astype(jnp.bfloat16)
    mixed = jnp.dot(attn_normed, attn_proj, preferred_element_type=jnp.float32)
    query = mixed[..., :channels].astype(jnp.bfloat16)
    keys = mixed[..., channels : 2 * channels].astype(jnp.bfloat16)
    values = mixed[..., 2 * channels : 3 * channels].astype(jnp.bfloat16)
    attn_gate = jax.nn.sigmoid(mixed[..., 3 * channels :])
    local_bias = jnp.transpose(
        jnp.dot(attn_normed, bias_proj, preferred_element_type=jnp.float32), (2, 0, 1)
    ).astype(jnp.bfloat16)
    key_rows, value_rows = (
        lax.all_gather(keys, "ch", axis=1, tiled=True),
        lax.all_gather(values, "ch", axis=1, tiled=True),
    )
    gathered = lax.all_gather(local_bias, ("row", "ch"), axis=1, tiled=True)
    gathered = gathered.reshape(head_count, row_devices, col_devices, row_count, col_count)
    full_bias = jnp.transpose(gathered, (0, 1, 3, 2, 4)).reshape(head_count, tokens, tokens)
    own_bias = lax.dynamic_slice_in_dim(full_bias, col_offset, col_count, 1)
    my_bias = own_bias.astype(jnp.float32)
    key_term = (key_valid - 1.0) * 1000000000.0
    score_scale = head_size ** (-0.5)
    group = 4
    blocks = row_count // group

    def attend(block):
        query_part, key_part, value_part = block
        query_heads = query_part.reshape(group, col_count, head_count, head_size)
        key_heads = key_part.reshape(group, tokens, head_count, head_size)
        value_heads = value_part.reshape(group, tokens, head_count, head_size)
        logits = (
            jnp.einsum(
                "ijhd,ikhd->ihjk", query_heads, key_heads, preferred_element_type=jnp.float32
            )
            * score_scale
        )
        logits = logits + my_bias[None] + key_term[None, None, None, :]
        attn_weights = jax.nn.softmax(logits, axis=-1).astype(jnp.bfloat16)
        output = jnp.einsum(
            "ihjk,ikhd->ijhd", attn_weights, value_heads, preferred_element_type=jnp.float32
        )
        return output.reshape(group, col_count, channels)

    attended = lax.map(
        attend,
        (
            query.reshape(blocks, group, col_count, channels),
            key_rows.reshape(blocks, group, tokens, channels),
            value_rows.reshape(blocks, group, tokens, channels),
        ),
    )
    attended = attended.reshape(row_count, col_count, channels)
    gated = (attended * attn_gate).astype(jnp.bfloat16)
    return (
        updated.astype(jnp.float32) + jnp.dot(gated, attn_out, preferred_element_type=jnp.float32)
    ).astype(jnp.bfloat16)


def solution(mesh):
    placed = (P("row", "ch", None), P(), P(), P(), P(), P(), P(), P(), P())
    return jax.shard_map(
        local, mesh=mesh, in_specs=placed, out_specs=P("row", "ch", None), check_vma=False
    )
```

profile of v0, /device:TPU:1, one launch (start us, length us, event | category | flops | bytes accessed | tf_op | source)
XLA Modules:
  0.0 354.2 jit_solution(14521930335235960371)
XLA Ops:
  6.5 1.4 copy.29
  8.9 1.3 fusion.27
  10.3 0.8 multiply_convert_fusion
  11.1 1.1 fusion.51
  12.2 0.4 copy.35
  12.7 75.9 %all-gather.5.cloned.1.call-done = bf16[512,128,128]{2,1,0:T(8,128)(2,1)} async-done(((bf16[16,128,128]{2,1,0:T(8,128)(2,1)}), bf16[512,128,128]{2,1,0:T(8,128)(2,1)}) %all-gather.5.cloned.1.call-update) | async-done | bytes 16777232 | tf_op jit(solution)/shard_map/all_gather | solution.py:43
  88.6 22.5 %copy.34 = bf16[512,128,128]{1,0,2:T(8,128)(2,1)} copy(bf16[512,128,128]{2,1,0:T(8,128)(2,1)} %all-gather.5.cloned.1.call-done) | data formatting | bytes 33554432 | tf_op jit(solution)/shard_map/all_gather | solution.py:43
  111.0 9.4 %convolution_bitcast_fusion = f32[16,512,128]{1,0,2:T(8,128)} fusion(bf16[512,128,128]{1,0,2:T(8,128)(2,1)} %copy.34, bf16[16,128,128]{1,0,2:T(8,128)(2,1)S(1)} %copy.35), kind=kOutput, calls=%fused_computation.18 | convolution fusion | flops 268435456 | bytes 21495808 | tf_op jit(solution)/shard_map/ikc,jkc->ijc/dot_general | solution.py:40
  120.5 45.9 %reduce-scatter.2.cloned.1.call-done = f32[16,128,128]{1,0,2:T(8,128)} async-done(((f32[16,512,128]{1,0,2:T(8,128)}), f32[16,128,128]{1,0,2:T(8,128)}) %reduce-scatter.2.cloned.1.call-update) | async-done | bytes 1048592 | tf_op jit(solution)/shard_map/reduce_scatter | solution.py:46
  166.4 1.4 reduce_sum.65
  167.8 1.4 multiply_reduce_fusion
  169.2 1.3 multiply_convert_fusion.1
  170.9 0.6 convert_reduce_fusion
  171.7 0.8 fusion.21
  172.6 2.7 fusion.52
  175.3 1.4 fusion.50
  177.0 0.4 all-gather.9.cloned.1.call-update
  177.4 1.3 slice.32
  178.7 1.3 copy.62
  180.0 58.1 %all-gather.11.cloned.1.call-done = bf16[4,2048,128]{2,0,1:T(4,128)(2,1)} async-done(((bf16[4,16,128]{2,0,1:T(4,128)(2,1)}), bf16[4,2048,128]{2,0,1:T(4,128)(2,1)}) %all-gather.11.cloned.1.call-update) | async-done | bytes 2097168 | tf_op jit(solution)/shard_map/all_gather | solution.py:65
  238.1 3.2 copy.40
  241.3 2.2 reshape.115
  243.5 2.2 dynamic-slice_convert_fusion
  245.7 21.8 %all-gather.7.cloned.1.call-done = bf16[16,512,128]{2,1,0:T(8,128)(2,1)} async-done(((bf16[16,128,128]{2,1,0:T(8,128)(2,1)}), bf16[16,512,128]{2,1,0:T(8,128)(2,1)}) %all-gather.7.cloned.1.call-update) | async-done | bytes 2097168 | tf_op jit(solution)/shard_map/all_gather | solution.py:63
  267.5 32.5 %all-gather.9.cloned.1.call-done = bf16[16,512,128]{2,1,0:T(8,128)(2,1)} async-done(((bf16[16,128,128]{2,1,0:T(8,128)(2,1)}), bf16[16,512,128]{2,1,0:T(8,128)(2,1)}) %all-gather.9.cloned.1.call-update) | async-done | bytes 2097168 | tf_op jit(solution)/shard_map/all_gather | solution.py:62
  300.0 44.4 %while.11 = (s32[]{:T(128)}, f32[4,4,128,128]{2,3,1,0:T(8,128)}, bf16[4,4,512,128]{3,2,1,0:T(8,128)(2,1)}, bf16[4,4,128,128]{3,2,1,0:T(8,128)(2,1)S(1)}, bf16[4,...) while((s32[]{:T(128)}, f32[4,4,128,128]{2,3,1,0:T(8,128)}, ...), condition=%wide.region_10.11_spmd.clone, body=%wide.region_7.10_spmd.clone.sunk | while | flops 141560320 | bytes 16142945 | solution.py:93
  300.0 1.3 constant_dynamic-slice_fusion.5
  301.7 0.7 add_multiply_fusion.2
  302.3 4.7 %fusion.69 = (f32[4,4,128]{2,1,0:T(4,128)S(1)}, f32[4,4,128,512]{3,2,1,0:T(8,128)}) fusion(f32[512]{0:T(512)S(1)} %add_multiply_fusion.2, f32[4,128,512]{2,1,0:T(8,128)} %get-tuple-element.175, bf16[4,128,4,32]{1,3,2,0:T(8,128)(2,1)S(1)} %bitcast.75, bf16[4,512,4,32]{1,3,2,0:T(8,128)(2,1)S(1)} %bitcast.70), kind=kOutput, calls=%fused_computation.74.clone.1 | convolution fusion | flops 72352256 | bytes 5908480 | tf_op jit(solution)/shard_map/while/body/eval_jaxpr/sub | solution.py:87
  307.3 3.1 fusion.70
  310.4 0.7 constant_dynamic-update-slice_fusion.2
  311.1 1.3 constant_dynamic-slice_fusion.5
  312.8 0.7 add_multiply_fusion.2
  313.4 4.7 %fusion.69 = (f32[4,4,128]{2,1,0:T(4,128)S(1)}, f32[4,4,128,512]{3,2,1,0:T(8,128)}) fusion(f32[512]{0:T(512)S(1)} %add_multiply_fusion.2, f32[4,128,512]{2,1,0:T(8,128)} %get-tuple-element.175, bf16[4,128,4,32]{1,3,2,0:T(8,128)(2,1)S(1)} %bitcast.75, bf16[4,512,4,32]{1,3,2,0:T(8,128)(2,1)S(1)} %bitcast.70), kind=kOutput, calls=%fused_computation.74.clone.1 | convolution fusion | flops 72352256 | bytes 5908480 | tf_op jit(solution)/shard_map/while/body/eval_jaxpr/sub | solution.py:87
  318.4 3.1 fusion.70
  321.4 0.8 constant_dynamic-update-slice_fusion.2
  322.2 1.3 constant_dynamic-slice_fusion.5
  323.9 0.7 add_multiply_fusion.2
  324.5 4.8 %fusion.69 = (f32[4,4,128]{2,1,0:T(4,128)S(1)}, f32[4,4,128,512]{3,2,1,0:T(8,128)}) fusion(f32[512]{0:T(512)S(1)} %add_multiply_fusion.2, f32[4,128,512]{2,1,0:T(8,128)} %get-tuple-element.175, bf16[4,128,4,32]{1,3,2,0:T(8,128)(2,1)S(1)} %bitcast.75, bf16[4,512,4,32]{1,3,2,0:T(8,128)(2,1)S(1)} %bitcast.70), kind=kOutput, calls=%fused_computation.74.clone.1 | convolution fusion | flops 72352256 | bytes 5908480 | tf_op jit(solution)/shard_map/while/body/eval_jaxpr/sub | solution.py:87
  329.5 3.1 fusion.70
  332.6 0.8 constant_dynamic-update-slice_fusion.2
  333.3 1.3 constant_dynamic-slice_fusion.5
  335.0 0.7 add_multiply_fusion.2
  335.6 4.8 %fusion.69 = (f32[4,4,128]{2,1,0:T(4,128)S(1)}, f32[4,4,128,512]{3,2,1,0:T(8,128)}) fusion(f32[512]{0:T(512)S(1)} %add_multiply_fusion.2, f32[4,128,512]{2,1,0:T(8,128)} %get-tuple-element.175, bf16[4,128,4,32]{1,3,2,0:T(8,128)(2,1)S(1)} %bitcast.75, bf16[4,512,4,32]{1,3,2,0:T(8,128)(2,1)S(1)} %bitcast.70), kind=kOutput, calls=%fused_computation.74.clone.1 | convolution fusion | flops 72352256 | bytes 5908480 | tf_op jit(solution)/shard_map/while/body/eval_jaxpr/sub | solution.py:87
  340.6 3.1 fusion.70
  343.7 0.7 constant_dynamic-update-slice_fusion.2
  344.4 1.9 fusion.26
  346.6 1.0 copy.47
  (53 shorter events, 3.9 us)
Async XLA Ops:
  6.5 166.1 %copy-start = (bf16[128,512]{1,0:T(8,128)(2,1)S(1)}, bf16[128,512]{1,0:T(8,128)(2,1)}, u32[]{:S(2)}) copy-start(bf16[128,512]{1,0:T(8,128)(2,1)} %param.17) | copy-start | bytes 393220
  6.5 3.7 %copy-start.4 = (bf16[128,256]{1,0:T(8,128)(2,1)S(1)}, bf16[128,256]{1,0:T(8,128)(2,1)}, u32[]{:S(2)}) copy-start(bf16[128,256]{1,0:T(8,128)(2,1)} %param.14) | copy-start | bytes 196612
  6.5 82.0 %all-gather.5.cloned.1.call-start = ((), (), s32[]{:S(2)}) async-start(), calls=%async_computation.1 | async-start | bytes 17301504 | tf_op jit(solution)/shard_map/all_gather | solution.py:43
  12.2 154.2 %reduce-scatter.2.cloned.1.call-start = ((), (), s32[]{:S(2)}) async-start(), calls=%async_computation.2 | async-start | bytes 5242880 | tf_op jit(solution)/shard_map/reduce_scatter | solution.py:46
  120.4 50.1 %copy-start.2 = (bf16[128,128]{1,0:T(8,128)(2,1)S(1)}, bf16[128,128]{1,0:T(8,128)(2,1)}, u32[]{:S(2)}) copy-start(bf16[128,128]{1,0:T(8,128)(2,1)} %param.16) | copy-start | bytes 98308
  120.4 50.5 %copy-start.5 = (bf16[128,128]{1,0:T(8,128)(2,1)S(1)}, bf16[128,128]{1,0:T(8,128)(2,1)}, u32[]{:S(2)}) copy-start(bf16[128,128]{1,0:T(8,128)(2,1)} %param.15) | copy-start | bytes 98308
  120.4 117.6 %all-gather.11.cloned.1.call-start = ((), (), s32[]{:S(2)}) async-start(), calls=%async_computation.5 | async-start | bytes 2113536 | tf_op jit(solution)/shard_map/all_gather | solution.py:65
  170.5 1.2 copy-start.6
  172.6 95.0 %all-gather.7.cloned.1.call-start = ((), (), s32[]{:S(2)}) async-start(), calls=%async_computation.3 | async-start | bytes 2621440 | tf_op jit(solution)/shard_map/all_gather | solution.py:63
  176.8 123.2 %all-gather.9.cloned.1.call-start = ((), (), s32[]{:S(2)}) async-start(), calls=%async_computation.4 | async-start | bytes 2621440 | tf_op jit(solution)/shard_map/all_gather | solution.py:62
  300.0 46.3 %copy-start.3 = (bf16[128,128]{1,0:T(8,128)(2,1)S(1)}, bf16[128,128]{1,0:T(8,128)(2,1)}, u32[]{:S(2)}) copy-start(bf16[128,128]{1,0:T(8,128)(2,1)} %param.19) | copy-start | bytes 98308
  344.4 3.2 copy-start.1
Sparse Core Ops, SparseCore 0:
  12.3 76.2 all-gather.4
  120.6 45.7 reduce-scatter.1
  172.7 65.3 all-gather.10
  239.7 27.7 all-gather.6
  269.1 30.8 all-gather.8
where the time goes:
time: 356 us; the launch traced here: 354 us
  waiting for transfers between devices  235 us (66%)
  matrix products  47.5 us (13%)
  local copies, waits for them, and re-layouts  46.2 us (13%)
  between operations  14 us (4%)
  other arithmetic  11.3 us (3%)
    all_gather x1, waiting for transfers between devices, local(): lax.all_gather(right_edges, 'row', axis=0, tiled=True)  75.9 us
    all_gather x1, waiting for transfers between devices, local(): gathered = lax.all_gather(local_bias, ('row', 'ch'), axis=1, tiled=True)  58.1 us
    reduce_scatter x1, waiting for transfers between devices, local(): lax.psum_scatter(partial_sums, 'ch', scatter_dimension=1, tiled=True)  45.9 us
    all_gather x1, waiting for transfers between devices, local(): lax.all_gather(keys, 'ch', axis=1, tiled=True)  32.5 us
    all_gather x1, local copies, waits for them, and re-layouts, local(): lax.all_gather(right_edges, 'row', axis=0, tiled=True)  22.5 us
    all_gather x1, waiting for transfers between devices, local(): lax.all_gather(values, 'ch', axis=1, tiled=True)  21.8 us
    sub x4, matrix products, attend(): attn_weights = jax.nn.softmax(logits, axis=-1).astype(jnp.bfloat16)  19 us
    dot_general x4, matrix products, attend(): jnp.einsum('ihjk,ikhd->ijhd', attn_weights, value_heads, preferred_elemen...  12.2 us
  transfers between devices with their start and end apart: 5, of which 5 were waited for; matrix products, arithmetic and copies ran while one was open for 4% of the time, Pallas kernels for 0%

commit v1 on v0

v1 whole, which is shorter than its diff:
```python
import functools
import math

import jax
import jax.numpy as jnp
from jax import lax
from jax.experimental import pallas as pl
from jax.experimental.pallas import tpu as pltpu
from jax.sharding import PartitionSpec as P

MESH = pl.DeviceIdType.MESH
EPS = 1e-05
F32 = jnp.float32
BF16 = jnp.bfloat16
LOG2E = math.log2(math.e)
NT = (((1,), (1,)), ((), ()))
NN = (((1,), (0,)), ((), ()))

LINE = 4
ROWS = 16
COLS = 128
CH = 128
TOK = 512
HEADS = 4
HEAD = 32
OWN = 4
DEVICES = 128


def dot(a, b, dims=NN):
    return lax.dot_general(a, b, dims, preferred_element_type=F32)


def sigmoid(x):
    return 0.5 * jnp.tanh(0.5 * x) + 0.5


def layer_norm(x):
    centre = x - jnp.mean(x, axis=-1, keepdims=True)
    spread = jnp.mean(centre * centre, axis=-1, keepdims=True)
    return centre * lax.rsqrt(spread + EPS)


def kernel(
    count_ref, pa, ep, eg, tg, to, ap, bp, ao,
    out,
    wt, ebuf, esend, lr, tst, tsend, trecv, tn, gbuf, a2, upd, an, qs, ks, vs, gs, bg, bias, osend,
    pa_send, pa_recv, pa_own, e_send, e_recv, t_send, t_recv,
    bx_send, bx_recv, by_send, by_recv, bz_send, bz_recv, bc_send, bc_recv, o_send, o_recv,
):
    r = lax.axis_index("row")
    q = lax.axis_index("ch")
    me = r * LINE + q
    z = lax.div(r, 8)
    y = lax.rem(lax.div(r, 2), 4)
    core = lax.rem(r, 2)
    count = count_ref[0]

    def place(zz, yy, cc):
        return zz * 8 + yy * 2 + cc

    def peer(step):
        t = lax.rem(step * 37, DEVICES)
        qq = lax.rem(q + lax.rem(t, 4), 4)
        cc = lax.rem(core + lax.rem(lax.div(t, 4), 2), 2)
        yy = lax.rem(y + lax.rem(lax.div(t, 8), 4), 4)
        zz = lax.rem(z + lax.div(t, 32), 4)
        return place(zz, yy, cc), qq

    def remote(src, dst, send, recv, rr, qq):
        return pltpu.make_async_remote_copy(
            src_ref=src, dst_ref=dst, send_sem=send, recv_sem=recv,
            device_id=(rr, qq), device_id_type=MESH,
        )

    def settle(ref, sem):
        pltpu.make_async_copy(ref, ref, sem).wait()

    barrier = pltpu.get_barrier_semaphore()

    @pl.loop(1, DEVICES)
    def _(step):
        rr, qq = peer(step)
        pl.semaphore_signal(barrier, inc=1, device_id=(rr, qq), device_id_type=MESH)

    wt[0:256, :] = ep[...].astype(F32).T.astype(BF16)
    wt[256:512, :] = eg[...].astype(F32).T.astype(BF16)
    lane = lax.broadcasted_iota(jnp.int32, (1, 256), 1)

    @pl.loop(0, ROWS // 2)
    def _(pair):
        x = pa[pl.ds(pair * 2, 2)].reshape(256, CH).astype(F32)
        normed = layer_norm(x).astype(BF16)
        both = dot(wt[...], normed, NT)
        row_token = r * ROWS + pair * 2 + lane // 128
        col_token = q * COLS + lane % 128
        valid = jnp.where((row_token < count) & (col_token < count), 1.0, 0.0)
        edges = sigmoid(both[256:512]) * both[0:256] * valid
        for side in range(2):
            for k in range(2):
                ebuf[pl.ds(side * 16 + pair * 2 + k, 128, stride=32), :] = edges[
                    side * 128 : side * 128 + 128, k * 128 : k * 128 + 128
                ]

    @pl.loop(0, 8)
    def _(part):
        rows = pl.ds(pl.multiple_of(part * 512, 512), 512)
        esend[rows, :] = ebuf[rows, :].astype(BF16)

    pl.semaphore_wait(barrier, DEVICES - 1)

    @pl.loop(1, DEVICES)
    def _(step):
        rr, qq = peer(step)
        rows = pl.ds(pl.multiple_of((rr * LINE + qq) * 32, 32), 32)
        remote(esend.at[rows], lr.at[q, r], e_send, e_recv, rr, qq).start()

    own = pl.ds(pl.multiple_of(me * 32, 32), 32)
    pltpu.make_async_copy(esend.at[own], lr.at[q, r], e_recv).start()

    pa_copies = []
    for dq in range(1, LINE):
        qq = lax.rem(q + dq, LINE)
        copy = remote(
            pa.at[pl.ds(qq * OWN, OWN)], a2.at[q], pa_send.at[dq - 1], pa_recv.at[dq - 1], r, qq
        )
        copy.start()
        pa_copies.append(copy)
    pa_local = pltpu.make_async_copy(pa.at[pl.ds(q * OWN, OWN)], a2.at[q], pa_own)
    pa_local.start()

    settle(lr, e_recv)
    right = jnp.concatenate([lr[k, :, 16:32, :].reshape(TOK, COLS) for k in range(LINE)], axis=1)
    for half in range(2):
        left = jnp.concatenate(
            [lr[k, half * 16 : half * 16 + 16, 0:16, :].reshape(256, COLS) for k in range(LINE)],
            axis=1,
        )
        tri = dot(left, right, NT)
        for jb in range(LINE):
            tst[pl.ds(half * 1024 + jb, 256, stride=4), :] = tri[:, jb * 128 : jb * 128 + 128]

    @pl.loop(0, 4)
    def _(part):
        rows = pl.ds(pl.multiple_of(part * 512, 512), 512)
        tsend[rows, :] = tst[rows, :].astype(BF16)

    @pl.loop(1, DEVICES)
    def _(step):
        rr, qq = peer(step)
        rows = pl.ds(pl.multiple_of((rr * LINE + qq) * 16, 16), 16)
        remote(tsend.at[rows], trecv.at[me], t_send, t_recv, rr, qq).start()

    own = pl.ds(pl.multiple_of(me * 16, 16), 16)
    pltpu.make_async_copy(tsend.at[own], trecv.at[me], t_recv).start()

    pa_local.wait()
    for copy in pa_copies:
        copy.wait()

    @pl.loop(0, OWN)
    def _(il):
        x = a2[:, il].reshape(TOK, CH).astype(F32)
        gbuf[il] = sigmoid(dot(layer_norm(x).astype(BF16), tg[...]))

    settle(trecv, t_recv)

    def add(part, total):
        return total + jnp.sum(trecv[pl.ds(part * 16, 16)].astype(F32), axis=0)

    mean = lax.fori_loop(0, 8, add, jnp.zeros((16, 128), F32)) * (1.0 / CH)

    def add_square(part, total):
        centre = trecv[pl.ds(part * 16, 16)].astype(F32) - mean[None]
        return total + jnp.sum(centre * centre, axis=0)

    spread = lax.fori_loop(0, 8, add_square, jnp.zeros((16, 128), F32)) * (1.0 / CH)
    gain = lax.rsqrt(spread + EPS)

    @pl.loop(0, 8)
    def _(part):
        block = (trecv[pl.ds(part * 16, 16)].astype(F32) - mean[None]) * gain[None]
        tn[pl.ds(pl.multiple_of(part * 256, 256), 256), :] = block.reshape(256, 128)

    spot = lax.broadcasted_iota(jnp.int32, (16, HEADS), 0) % HEADS
    pick = (spot == lax.broadcasted_iota(jnp.int32, (16, HEADS), 1)).astype(BF16)
    bias_w = dot(pick, bp[...], NT).astype(BF16)
    bias_row = lax.broadcasted_iota(jnp.int32, (16, TOK), 0) // HEADS

    def update(il, own_bias):
        blocks = [
            tn[pl.ds(il * LINE + jb, 128, stride=16), :].T.astype(BF16) for jb in range(LINE)
        ]
        product = dot(jnp.concatenate(blocks, axis=0), to[...])
        x = a2[:, il].reshape(TOK, CH).astype(F32)
        updated = (x + gbuf[il] * product).astype(BF16)
        upd[il] = updated
        normed = layer_norm(updated.astype(F32)).astype(BF16)
        an[il] = normed
        return jnp.where(bias_row == il, dot(bias_w, normed, NT), own_bias)

    own_bias = lax.fori_loop(0, OWN, update, jnp.zeros((16, TOK), F32)).astype(BF16)
    for kb in range(LINE):
        bg[z, core, y, q, kb * 16 : kb * 16 + 16, :] = own_bias[:, kb * 128 : kb * 128 + 128]

    sends = []
    for dq in range(1, LINE):
        copy = remote(
            bg.at[z, core, y, q], bg.at[z, core, y, q], bx_send.at[dq - 1], bx_recv.at[dq - 1],
            r, lax.rem(q + dq, LINE),
        )
        copy.start()
        sends.append(copy)

    def project(il):
        mixed = dot(an[il], ap[...])
        qs[il] = (mixed[:, 0:CH] * (HEAD**-0.5 * LOG2E)).astype(BF16)
        ks[il] = mixed[:, CH : 2 * CH].astype(BF16)
        vs[il] = mixed[:, 2 * CH : 3 * CH].astype(BF16)
        gs[il] = sigmoid(mixed[:, 3 * CH : 4 * CH])

    @pl.loop(0, 2)
    def _(il):
        project(il)

    for dq in range(1, LINE):
        slot = bg.at[z, core, y, lax.rem(q + LINE - dq, LINE)]
        settle(slot, bx_recv.at[dq - 1])
    twin = place(z, y, 1 - core)
    for dy in range(1, LINE):
        copy = remote(
            bg.at[z, core, y], bg.at[z, core, y], by_send.at[dy - 1], by_recv.at[dy - 1],
            place(z, lax.rem(y + dy, LINE), core), q,
        )
        copy.start()
        sends.append(copy)
    copy = remote(bg.at[z, core, y], bg.at[z, core, y], bc_send.at[0], bc_recv.at[0], twin, q)
    copy.start()
    sends.append(copy)

    @pl.loop(2, OWN)
    def _(il):
        project(il)

    for dy in range(1, LINE):
        yy = lax.rem(y + LINE - dy, LINE)
        settle(bg.at[z, core, yy], by_recv.at[dy - 1])
        copy = remote(
            bg.at[z, core, yy], bg.at[z, core, yy], bc_send.at[dy], bc_recv.at[dy], twin, q
        )
        copy.start()
        sends.append(copy)
    for dz in range(1, LINE):
        copy = remote(
            bg.at[z, core], bg.at[z, core], bz_send.at[dz - 1], bz_recv.at[dz - 1],
            place(lax.rem(z + dz, LINE), y, core), q,
        )
        copy.start()
        sends.append(copy)
    for dy in range(LINE):
        settle(bg.at[z, 1 - core, lax.rem(y + LINE - dy, LINE)], bc_recv.at[dy])

    key_lane = lax.broadcasted_iota(jnp.int32, (1, TOK), 1)
    key_term = jnp.where(key_lane < count, 0.0, -1e9 * LOG2E)
    head_of = lax.broadcasted_iota(jnp.int32, (128, CH), 1) // HEAD

    def forward(dz):
        zz = lax.rem(z + LINE - dz, LINE)
        return remote(
            bg.at[zz, core], bg.at[zz, core], bc_send.at[3 + dz], bc_recv.at[3 + dz], twin, q
        )

    @pl.loop(0, LINE)
    def _(step):
        jb = lax.rem(z + LINE - step, LINE)

        @pl.when(step > 0)
        def _():
            settle(bg.at[jb, 1 - core], bc_recv.at[3 + step])

        @pl.loop(0, LINE)
        def _(yy):
            for cc in range(2):
                for xx in range(LINE):
                    rows = pl.ds(pl.multiple_of(yy * 128 + cc * 64 + xx * 16, 16), 16)
                    tile = bg[jb, cc, yy, xx].astype(F32)
                    for kb in range(LINE):
                        cols = slice(kb * 128, kb * 128 + 128)
                        bias[kb, rows, :] = tile[kb * 16 : kb * 16 + 16] * LOG2E + key_term[:, cols]

        @pl.loop(0, OWN)
        def _(il):
            @pl.when((il == 2) & (step < LINE - 1))
            def _():
                zz = lax.rem(z + LINE - 1 - step, LINE)
                settle(bg.at[zz, core], bz_recv.at[step])
                forward(step + 1).start()

            block = pl.ds(pl.multiple_of(jb * 128, 128), 128)
            query = qs[il, block, :]
            masked = [jnp.where(head_of == h, query, jnp.zeros_like(query)) for h in range(HEADS)]
            scores = dot(jnp.concatenate(masked, axis=0), ks[il], NT)
            weights = []
            scale = []
            for h in range(HEADS):
                own = [bias[kb, pl.ds(h, 128, stride=4), :] for kb in range(LINE)]
                logits = scores[h * 128 : h * 128 + 128] + jnp.concatenate(own, axis=1)
                powers = jnp.exp2(logits - jnp.max(logits, axis=-1, keepdims=True))
                scale.append(1.0 / jnp.sum(powers, axis=-1, keepdims=True))
                weights.append(powers.astype(BF16))
            mixed = dot(jnp.concatenate(weights, axis=0), vs[il])
            attended = jnp.zeros((128, CH), F32)
            for h in range(HEADS):
                attended = jnp.where(head_of == h, mixed[h * 128 : h * 128 + 128] * scale[h], attended)
            gated = (attended * gs[il, block, :]).astype(BF16)
            result = upd[il, block, :].astype(F32) + dot(gated, ao[...])
            osend[jb, il] = result.astype(BF16)

            target = out.at[q * OWN + il]

            @pl.when(jb != q)
            def _():
                remote(osend.at[jb, il], target, o_send, o_recv, r, jb).start()

            @pl.when(jb == q)
            def _():
                pltpu.make_async_copy(osend.at[jb, il], target, o_recv).start()

    settle(out, o_recv)
    settle(osend.at[0:3], o_send)
    settle(esend.at[0 : 32 * (DEVICES - 1)], e_send)
    settle(tsend.at[0 : 16 * (DEVICES - 1)], t_send)
    for copy in sends:
        copy.wait_send()
    for dz in range(1, LINE):
        forward(dz).wait_send()


def local(pair_act, valid_count, edge_proj, edge_gate, tri_gate, tri_out, attn_proj, bias_proj, attn_out):
    vmem = pl.BlockSpec(memory_space=pltpu.VMEM)
    dma = pltpu.SemaphoreType.DMA
    return pl.pallas_call(
        kernel,
        out_shape=jax.ShapeDtypeStruct((ROWS, COLS, CH), BF16),
        in_specs=[pl.BlockSpec(memory_space=pltpu.SMEM)] + [vmem] * 8,
        out_specs=pl.BlockSpec(memory_space=pl.ANY),
        scratch_shapes=[
            pltpu.VMEM((512, CH), BF16),
            pltpu.VMEM((4096, COLS), F32),
            pltpu.VMEM((4096, COLS), BF16),
            pltpu.VMEM((LINE, 32, 32, COLS), BF16),
            pltpu.VMEM((2048, 128), F32),
            pltpu.VMEM((2048, 128), BF16),
            pltpu.VMEM((CH, 16, 128), BF16),
            pltpu.VMEM((2048, 128), F32),
            pltpu.VMEM((OWN, TOK, CH), F32),
            pltpu.VMEM((LINE, OWN, COLS, CH), BF16),
            pltpu.VMEM((OWN, TOK, CH), BF16),
            pltpu.VMEM((OWN, TOK, CH), BF16),
            pltpu.VMEM((OWN, TOK, CH), BF16),
            pltpu.VMEM((OWN, TOK, CH), BF16),
            pltpu.VMEM((OWN, TOK, CH), BF16),
            pltpu.VMEM((OWN, TOK, CH), F32),
            pltpu.VMEM((LINE, 2, LINE, LINE, 64, 128), BF16),
            pltpu.VMEM((LINE, 512, 128), F32),
            pltpu.VMEM((LINE, OWN, 128, CH), BF16),
            dma((3,)), dma((3,)), dma, dma, dma, dma, dma,
            dma((3,)), dma((3,)), dma((3,)), dma((3,)), dma((3,)), dma((3,)), dma((7,)), dma((7,)),
            dma, dma,
        ],
        compiler_params=pltpu.CompilerParams(
            collective_id=0, has_side_effects=True, vmem_limit_bytes=48 * 1024 * 1024
        ),
        name="triangle",
    )(valid_count, pair_act, edge_proj, edge_gate, tri_gate, tri_out, attn_proj, bias_proj, attn_out)


def solution(mesh):
    placed = (P("row", "ch", None), P(), P(), P(), P(), P(), P(), P(), P())
    return jax.shard_map(
        local, mesh=mesh, in_specs=placed, out_specs=P("row", "ch", None), check_vma=False
    )
```

time: 356 us -> 87.3 us (0.25)
  the two profiles are of different devices: /device:TPU:1 before, /device:TPU:3 now
where the time goes in v1:
time: 87.3 us; the launch traced here: 86.9 us
  Pallas kernels  80.1 us (92%)
  local copies, waits for them, and re-layouts  6.08 us (7%)
    pallas_call x1, Pallas kernels, local(): pl.pallas_call(kernel, out_shape=jax.ShapeDtypeStruct((ROWS, COLS, CH), B...  80.1 us
    unnamed x18, local copies, waits for them, and re-layouts  6.08 us

profile of v1, /device:TPU:3, one launch (start us, length us, event | category | flops | bytes accessed | tf_op | source)
XLA Modules:
  0.0 86.9 jit_solution(13530562271112097930)
XLA Ops:
  0.0 0.0 copy-start.7
  0.0 0.0 copy-start.4
  0.7 0.0 copy-done.7
  0.7 0.1 copy.10.bp
  0.8 0.0 copy-done.4
  0.8 0.0 copy-start
  0.8 1.0 %copy-done = bf16[16,128,128]{2,1,0:T(8,128)(2,1)S(1)} copy-done((bf16[16,128,128]{2,1,0:T(8,128)(2,1)S(1)}, bf16[16,128,128]{2,1,0:T(8,128)(2,1)}, u32[]{:S(2)}) %copy-start) | copy-done | bytes 524312
  1.9 0.0 copy-start.1
  1.9 0.9 %copy-done.1 = bf16[128,512]{1,0:T(8,128)(2,1)S(1)} copy-done((bf16[128,512]{1,0:T(8,128)(2,1)S(1)}, bf16[128,512]{1,0:T(8,128)(2,1)}, u32[]{:S(2)}) %copy-start.1) | copy-done | bytes 131096
  2.8 0.0 copy-start.2
  2.8 0.8 copy-done.2
  3.6 0.0 copy-start.3
  3.6 0.8 copy-done.3
  4.5 0.0 copy-start.5
  4.5 0.8 copy-done.5
  5.2 0.0 copy-start.6
  5.2 0.8 copy-done.6
  6.0 80.1 %triangle.1 = bf16[16,128,128]{2,1,0:T(8,128)(2,1)S(1)} custom-call(s32[1]{0:T(128)S(6)} %copy.12.count_ref, bf16[16,128,128]{2,1,0:T(8,128)(2,1)S(1)} %copy-done, bf16[128,256]{1,0:T(8,128)(2,1)S(1)} %copy-done.2, bf16[128,256]{1,0:T(8,128)(2,1)S(1)} %copy-done.3, bf16[128,128]{1,0:T(8,128)(2,1)S(1)} %copy-done.4, bf16[128,128]{1,0:T(8,128)(2,1)S(1)} %copy-done.5, ...), custom_call_target="tpu_custom_call" | custom-call | tf_op jit(solution)/shard_map/triangle/pallas_call | solution.py:342
  86.1 0.8 copy.13
Async XLA Ops:
  0.0 0.7 copy-start.7
  0.0 0.8 copy-start.4
  0.8 1.0 %copy-start = (bf16[16,128,128]{2,1,0:T(8,128)(2,1)S(1)}, bf16[16,128,128]{2,1,0:T(8,128)(2,1)}, u32[]{:S(2)}) copy-start(bf16[16,128,128]{2,1,0:T(8,128)(2,1)} %pa.1) | copy-start | bytes 1572868
  1.9 0.9 %copy-start.1 = (bf16[128,512]{1,0:T(8,128)(2,1)S(1)}, bf16[128,512]{1,0:T(8,128)(2,1)}, u32[]{:S(2)}) copy-start(bf16[128,512]{1,0:T(8,128)(2,1)} %ap.1) | copy-start | bytes 393220
  2.8 0.8 copy-start.2
  3.6 0.8 copy-start.3
  4.5 0.8 copy-start.5
  5.2 0.8 copy-start.6

commit v2 on v1

v2 whole, which is shorter than its diff:
```python
import math

import jax
import jax.numpy as jnp
from jax import lax
from jax.experimental import pallas as pl
from jax.experimental.pallas import tpu as pltpu
from jax.sharding import PartitionSpec as P

MESH = pl.DeviceIdType.MESH
EPS = 1e-05
F32 = jnp.float32
BF16 = jnp.bfloat16
LOG2E = math.log2(math.e)
NT = (((1,), (1,)), ((), ()))
NN = (((1,), (0,)), ((), ()))

LINE = 4
ROWS = 16
COLS = 128
CH = 128
TOK = 512
HEADS = 4
HEAD = 32
OWN = 4
DEVICES = 128


OFFSETS = [
    (dz, dy, dc, dx) for dz in range(LINE) for dy in range(LINE) for dc in range(2) for dx in range(LINE)
][1:]


def hops(offset):
    dz, dy, _, dx = offset
    return sum(min(d, LINE - d) for d in (dz, dy, dx))


FAR_FIRST = sorted(OFFSETS, key=hops, reverse=True)


def dot(a, b, dims=NN):
    return lax.dot_general(a, b, dims, preferred_element_type=F32)


def sigmoid(x):
    return 0.5 * jnp.tanh(0.5 * x) + 0.5


def layer_norm(x):
    centre = x - jnp.mean(x, axis=-1, keepdims=True)
    spread = jnp.mean(centre * centre, axis=-1, keepdims=True)
    return centre * lax.rsqrt(spread + EPS)


def kernel(
    count_ref, pa_in, ep_in, eg_in, tg_in, to_in, ap_in, bp_in, ao_in,
    out,
    pa, ep, eg, tg, to, ap, bp, ao, wt, nrm, ebuf, esend, lr, tst, tsend, trecv, tn, gbuf, a2, upd, an, qs, ks, vs, gs, ba, bb, bc, sbuf, bias, osend,
    ready, load, pa_send, pa_recv, pa_own, e_send, e_recv, t_send, t_recv,
    b_send, b_recv, u_send, u_recv, o_send, o_recv,
):
    r = lax.axis_index("row")
    q = lax.axis_index("ch")
    me = r * LINE + q
    z = lax.div(r, 8)
    y = lax.rem(lax.div(r, 2), 4)
    core = lax.rem(r, 2)
    count = count_ref[0]

    def place(zz, yy, cc):
        return zz * 8 + yy * 2 + cc

    zs = [lax.rem(z + d, LINE) for d in range(LINE)]
    ys = [lax.rem(y + d, LINE) for d in range(LINE)]
    xs = [lax.rem(q + d, LINE) for d in range(LINE)]
    cores = [core, 1 - core]

    def peer(offset):
        dz, dy, dc, dx = offset
        return place(zs[dz], ys[dy], cores[dc]), xs[dx]

    def remote(src, dst, send, recv, rr, qq):
        return pltpu.make_async_remote_copy(
            src_ref=src, dst_ref=dst, send_sem=send, recv_sem=recv,
            device_id=(rr, qq), device_id_type=MESH,
        )

    def settle(ref, sem):
        pltpu.make_async_copy(ref, ref, sem).wait()

    loads = [
        pltpu.make_async_copy(src, dst, load.at[n])
        for n, (src, dst) in enumerate(
            [(ep_in, ep), (eg_in, eg), (pa_in, pa), (tg_in, tg), (to_in, to), (ap_in, ap), (bp_in, bp), (ao_in, ao)]
        )
    ]
    for copy in loads:
        copy.start()

    barrier = pltpu.get_barrier_semaphore()

    plane = [o for o in OFFSETS if o[2] == 0 and o[3] == 0]
    near = [o for o in OFFSETS if o[0] == 0 and o[1] == 0] + plane
    for offset in near:
        rr, qq = peer(offset)
        pl.semaphore_signal(barrier, inc=1, device_id=(rr, qq), device_id_type=MESH)

    for copy in loads:
        copy.wait()

    @pl.loop(0, 4)
    def _(part):
        x = pa[pl.ds(part * 4, 4)].reshape(512, CH).astype(F32)
        nrm[pl.ds(pl.multiple_of(part * 512, 512), 512), :] = layer_norm(x).astype(BF16)

    pl.semaphore_wait(barrier, len(near))
    for offset in plane:
        rr, qq = peer(offset)
        pl.semaphore_signal(ready, inc=1, device_id=(rr, qq), device_id_type=MESH)

    spot = lax.broadcasted_iota(jnp.int32, (CH, CH), 0)
    line = spot % 32
    chosen = line * 4 + (spot // 32 + 8 - line // 8 - (line // 2) % 4) % 4
    order = (chosen == lax.broadcasted_iota(jnp.int32, (CH, CH), 1)).astype(BF16)
    for n, ref in enumerate((ep, ep, eg, eg)):
        side = n % 2
        part = dot(order, ref[:, side * CH : side * CH + CH], NT).astype(BF16)
        for m in range(4):
            wt[m, n * 32 : n * 32 + 32, :] = part[m * 32 : m * 32 + 32]
    lane = lax.broadcasted_iota(jnp.int32, (1, 512), 1)

    def edges_of(k):
        weights = wt[lax.rem(z + y + q + k, 4)]
        for part in range(4):
            both = dot(weights, nrm[part * 512 : part * 512 + 512, :], NT)
            row_token = r * ROWS + part * 4 + lane // 128
            col_token = q * COLS + lane % 128
            valid = jnp.where((row_token < count) & (col_token < count), 1.0, 0.0)
            edges = sigmoid(both[64:128]) * both[0:64] * valid
            for i in range(4):
                for side in range(2):
                    ebuf[pl.ds(side * 16 + part * 4 + i, 32, stride=36), :] = edges[
                        side * 32 : side * 32 + 32, i * 128 : i * 128 + 128
                    ]
        for n in range(32):
            esend[k, n * 32 : n * 32 + 32, :] = ebuf[n * 36 : n * 36 + 32, :].astype(BF16)

    for step, k in enumerate((2, 1, 3, 0)):
        edges_of(k)
        if step == 0:
            pl.semaphore_wait(ready, len(plane))
        for offset in FAR_FIRST:
            if (offset[0] + offset[1] + offset[3]) % 4 == k:
                rr, qq = peer(offset)
                rows = pl.ds(pl.multiple_of(rr * 32, 32), 32)
                remote(esend.at[k, rows], lr.at[q, r], e_send, e_recv, rr, qq).start()

    own = pl.ds(pl.multiple_of(r * 32, 32), 32)
    pltpu.make_async_copy(esend.at[0, own], lr.at[q, r], e_recv).start()

    pa_copies = []
    for dq in range(1, LINE):
        qq = lax.rem(q + dq, LINE)
        copy = remote(
            pa.at[pl.ds(qq * OWN, OWN)], a2.at[q], pa_send.at[dq - 1], pa_recv.at[dq - 1], r, qq
        )
        copy.start()
        pa_copies.append(copy)
    pa_local = pltpu.make_async_copy(pa.at[pl.ds(q * OWN, OWN)], a2.at[q], pa_own)
    pa_local.start()

    settle(lr, e_recv)
    right = jnp.concatenate([lr[k, :, 16:32, :].reshape(TOK, COLS) for k in range(LINE)], axis=1)
    for half in range(2):
        left = jnp.concatenate(
            [lr[k, half * 16 : half * 16 + 16, 0:16, :].reshape(256, COLS) for k in range(LINE)],
            axis=1,
        )
        tri = dot(left, right, NT)
        for jb in range(LINE):
            tst[pl.ds(half * 1024 + jb, 256, stride=4), :] = tri[:, jb * 128 : jb * 128 + 128]

    @pl.loop(0, 4)
    def _(part):
        rows = pl.ds(pl.multiple_of(part * 512, 512), 512)
        tsend[rows, :] = tst[rows, :].astype(BF16)

    for offset in FAR_FIRST:
        rr, qq = peer(offset)
        rows = pl.ds(pl.multiple_of((rr * LINE + qq) * 16, 16), 16)
        remote(tsend.at[rows], trecv.at[me], t_send, t_recv, rr, qq).start()

    own = pl.ds(pl.multiple_of(me * 16, 16), 16)
    pltpu.make_async_copy(tsend.at[own], trecv.at[me], t_recv).start()

    pa_local.wait()
    for copy in pa_copies:
        copy.wait()

    @pl.loop(0, OWN)
    def _(il):
        x = a2[:, il].reshape(TOK, CH).astype(F32)
        gbuf[il] = sigmoid(dot(layer_norm(x).astype(BF16), tg[...]))

    settle(trecv, t_recv)

    def add(part, total):
        return total + jnp.sum(trecv[pl.ds(part * 16, 16)].astype(F32), axis=0)

    mean = lax.fori_loop(0, 8, add, jnp.zeros((16, 128), F32)) * (1.0 / CH)

    def add_square(part, total):
        centre = trecv[pl.ds(part * 16, 16)].astype(F32) - mean[None]
        return total + jnp.sum(centre * centre, axis=0)

    spread = lax.fori_loop(0, 8, add_square, jnp.zeros((16, 128), F32)) * (1.0 / CH)
    gain = lax.rsqrt(spread + EPS)

    @pl.loop(0, 8)
    def _(part):
        block = (trecv[pl.ds(part * 16, 16)].astype(F32) - mean[None]) * gain[None]
        for n in range(16):
            tn[pl.ds(part * 320 + n * 20, 16), :] = block[n]

    spot = lax.broadcasted_iota(jnp.int32, (16, HEADS), 0) % HEADS
    pick = (spot == lax.broadcasted_iota(jnp.int32, (16, HEADS), 1)).astype(BF16)
    bias_w = dot(pick, bp[...]).astype(BF16)
    bias_row = lax.broadcasted_iota(jnp.int32, (16, TOK), 0) // HEADS

    def update(il, own_bias):
        blocks = [
            tn[pl.ds(il * LINE + jb, 128, stride=20), :].T.astype(BF16) for jb in range(LINE)
        ]
        product = dot(jnp.concatenate(blocks, axis=0), to[...])
        x = a2[:, il].reshape(TOK, CH).astype(F32)
        updated = (x + gbuf[il] * product).astype(BF16)
        upd[core * OWN + il] = updated.reshape(16, 2, 16, CH)
        normed = layer_norm(updated.astype(F32)).astype(BF16)
        an[il] = normed.reshape(16, 2, 16, CH)
        return jnp.where(bias_row == il, dot(bias_w, normed, NT), own_bias)

    own_bias = lax.fori_loop(0, OWN, update, jnp.zeros((16, TOK), F32)).astype(BF16)
    ba[z, y, q, 0:16, :] = own_bias[:, 0:128]
    ba[z, y, q, 16:32, :] = own_bias[:, 128:256]
    bb[y, q, z] = own_bias[:, 256:384]
    bc[q, z, y] = own_bias[:, 384:512]

    parts = [(ba, "zyx"), (bb, "yxz"), (bc, "xzy")]
    at = {"z": zs, "y": ys, "x": xs}

    def spread(stage):
        copies = []
        for n, (ref, axes) in enumerate(parts):
            slot = ref.at[tuple(at[axis][0] for axis in axes[: 3 - stage])]
            for d in range(1, LINE):
                offset = {"z": 0, "y": 0, "x": 0}
                offset[axes[2 - stage]] = d
                rr, qq = peer((offset["z"], offset["y"], 0, offset["x"]))
                sem = stage * 9 + n * 3 + d - 1
                copies.append(remote(slot, slot, b_send.at[sem], b_recv.at[sem], rr, qq))
        for copy in copies:
            copy.start()
        return copies

    def spread_wait(stage):
        for n, (ref, axes) in enumerate(parts):
            for d in range(1, LINE):
                place_of = [at[axis][0] for axis in axes[: 3 - stage]]
                place_of[-1] = at[axes[2 - stage]][LINE - d]
                settle(ref.at[tuple(place_of)], b_recv.at[stage * 9 + n * 3 + d - 1])

    copies = spread(0)
    twin = place(z, y, 1 - core)
    mine = pl.ds(core * OWN, OWN)
    theirs = pl.ds((1 - core) * OWN, OWN)
    swap = remote(upd.at[mine], upd.at[mine], u_send, u_recv, twin, q)
    swap.start()

    head_of = lax.broadcasted_iota(jnp.int32, (256, CH), 1) // HEAD

    def project(n, il):
        half = an[il, :, core].reshape(256, CH)
        qs[n] = (dot(half, ap[:, 0:CH]) * (HEAD**-0.5 * LOG2E)).astype(BF16)
        gs[n] = sigmoid(dot(half, ap[:, 3 * CH : 4 * CH]))
        mixed = dot(an[il].reshape(TOK, CH), ap[:, CH : 3 * CH])
        ks[n] = mixed[:, 0:CH].astype(BF16)
        vs[n, :, 0:CH] = mixed[:, CH : 2 * CH].astype(BF16)
        vs[n, :, CH : 2 * CH] = jnp.ones((TOK, CH), BF16)

    def score(n):
        query = qs[n]
        for pair in range(2):
            masked = [
                jnp.where(head_of == pair * 2 + h, query, jnp.zeros_like(query)) for h in range(2)
            ]
            sbuf[n, pair * 512 : pair * 512 + 512, :] = dot(jnp.concatenate(masked, axis=0), ks[n], NT)

    @pl.loop(0, OWN)
    def _(il):
        project(il, il)

    score(0)
    spread_wait(0)
    copies += spread(1)

    @pl.loop(1, OWN)
    def _(n):
        score(n)

    spread_wait(1)
    copies += spread(2)
    swap.wait_recv()

    @pl.loop(0, OWN)
    def _(il):
        normed = layer_norm(upd[(1 - core) * OWN + il].reshape(TOK, CH).astype(F32)).astype(BF16)
        an[il] = normed.reshape(16, 2, 16, CH)
        project(OWN + il, il)

    @pl.loop(OWN, 2 * OWN)
    def _(n):
        score(n)

    spread_wait(2)
    key_lane = lax.broadcasted_iota(jnp.int32, (1, TOK), 1)
    key_term = jnp.where(key_lane < count, 0.0, -1e9 * LOG2E)

    @pl.loop(0, LINE)
    def _(zz):
        for yy in range(LINE):
            for xx in range(LINE):
                rows = pl.ds(pl.multiple_of(zz * 256 + yy * 64 + xx * 16, 16), 16)
                tiles = [ba[zz, yy, xx, 0:16], ba[zz, yy, xx, 16:32], bb[yy, xx, zz], bc[xx, zz, yy]]
                for kb, tile in enumerate(tiles):
                    cols = slice(kb * 128, kb * 128 + 128)
                    bias[kb, rows, :] = tile.astype(F32) * LOG2E + key_term[:, cols]

    def attend(n, own_row):
        weights = []
        for h in range(HEADS):
            for part in range(4):
                rows = slice(h * 256 + part * 64, h * 256 + part * 64 + 64)
                own = [bias[kb, pl.ds(part * 256 + h, 64, stride=4), :] for kb in range(LINE)]
                logits = sbuf[n, rows, :] + jnp.concatenate(own, axis=1)
                powers = jnp.exp2(logits - jnp.max(logits, axis=-1, keepdims=True))
                weights.append(powers.astype(BF16))
        mixed = dot(jnp.concatenate(weights, axis=0), vs[n])
        total = mixed[0:256]
        for h in range(1, HEADS):
            mask = jnp.concatenate([head_of, head_of], axis=1) == h
            total = jnp.where(mask, mixed[h * 256 : h * 256 + 256], total)
        attended = total[:, 0:CH] / total[:, CH : 2 * CH]
        gated = (attended * gs[n]).astype(BF16)
        before = upd[own_row, :, core].reshape(256, CH).astype(F32)
        result = before + dot(gated, ao[...])
        osend[n] = result.astype(BF16).reshape(LINE, 4, 16, CH)

    @pl.loop(0, OWN)
    def _(il):
        attend(OWN + il, (1 - core) * OWN + il)
        for d in range(LINE):
            jb = xs[d]
            target = out.at[q * OWN + il, :, core]
            remote(osend.at[OWN + il, jb], target, o_send, o_recv, twin, jb).start()

    @pl.loop(0, OWN)
    def _(il):
        attend(il, core * OWN + il)
        target = out.at[q * OWN + il, :, core]
        for d in range(1, LINE):
            jb = xs[d]
            remote(osend.at[il, jb], target, o_send, o_recv, r, jb).start()
        pltpu.make_async_copy(osend.at[il, q], target, o_recv).start()

    settle(out, o_recv)
    settle(osend.at[0:7], o_send)
    settle(esend.at[0:3], e_send)
    settle(esend.at[0, 0 : 31 * 32], e_send)
    settle(tsend.at[0 : 16 * (DEVICES - 1)], t_send)
    swap.wait_send()
    for copy in copies:
        copy.wait_send()


def local(pair_act, valid_count, edge_proj, edge_gate, tri_gate, tri_out, attn_proj, bias_proj, attn_out):
    hbm = pl.BlockSpec(memory_space=pltpu.HBM)
    dma = pltpu.SemaphoreType.DMA
    return pl.pallas_call(
        kernel,
        out_shape=jax.ShapeDtypeStruct((ROWS, 4, 2, 16, CH), BF16),
        in_specs=[pl.BlockSpec(memory_space=pltpu.SMEM)] + [hbm] * 8,
        out_specs=pl.BlockSpec(memory_space=pl.ANY),
        scratch_shapes=[
            pltpu.VMEM((ROWS, COLS, CH), BF16),
            pltpu.VMEM((CH, 2 * CH), BF16),
            pltpu.VMEM((CH, 2 * CH), BF16),
            pltpu.VMEM((CH, CH), BF16),
            pltpu.VMEM((CH, CH), BF16),
            pltpu.VMEM((CH, 4 * CH), BF16),
            pltpu.VMEM((HEADS, CH), BF16),
            pltpu.VMEM((CH, CH), BF16),
            pltpu.VMEM((4, 128, CH), BF16),
            pltpu.VMEM((2048, CH), BF16),
            pltpu.VMEM((32 * 36, COLS), F32),
            pltpu.VMEM((4, 1024, COLS), BF16),
            pltpu.VMEM((LINE, 32, 32, COLS), BF16),
            pltpu.VMEM((2048, 128), F32),
            pltpu.VMEM((2048, 128), BF16),
            pltpu.VMEM((CH, 16, 128), BF16),
            pltpu.VMEM((CH * 20, 128), F32),
            pltpu.VMEM((OWN, TOK, CH), F32),
            pltpu.VMEM((LINE, OWN, COLS, CH), BF16),
            pltpu.VMEM((2 * OWN, 16, 2, 16, CH), BF16),
            pltpu.VMEM((OWN, 16, 2, 16, CH), BF16),
            pltpu.VMEM((2 * OWN, 256, CH), BF16),
            pltpu.VMEM((2 * OWN, TOK, CH), BF16),
            pltpu.VMEM((2 * OWN, TOK, 2 * CH), BF16),
            pltpu.VMEM((2 * OWN, 256, CH), F32),
            pltpu.VMEM((LINE, LINE, LINE, 32, 128), BF16),
            pltpu.VMEM((LINE, LINE, LINE, 16, 128), BF16),
            pltpu.VMEM((LINE, LINE, LINE, 16, 128), BF16),
            pltpu.VMEM((2 * OWN, 1024, TOK), F32),
            pltpu.VMEM((LINE, 1024, 128), F32),
            pltpu.VMEM((2 * OWN, LINE, 4, 16, CH), BF16),
            pltpu.SemaphoreType.REGULAR, dma((8,)), dma((3,)), dma((3,)), dma, dma, dma, dma, dma,
            dma((27,)), dma((27,)), dma, dma, dma, dma,
        ],
        compiler_params=pltpu.CompilerParams(
            collective_id=0, has_side_effects=True, vmem_limit_bytes=63 * 1024 * 1024
        ),
        name="triangle",
    )(valid_count, pair_act, edge_proj, edge_gate, tri_gate, tri_out, attn_proj, bias_proj.T, attn_out).reshape(ROWS, COLS, CH)


def solution(mesh):
    placed = (P("row", "ch", None), P(), P(), P(), P(), P(), P(), P(), P())
    return jax.shard_map(
        local, mesh=mesh, in_specs=placed, out_specs=P("row", "ch", None), check_vma=False
    )
```

time: 87.3 us -> 67.7 us (0.78)
  the two profiles are of different devices: /device:TPU:3 before, /device:TPU:0 now
where the time goes in v2:
time: 67.7 us; the launch traced here: 67.5 us
  Pallas kernels  65 us (96%)
  local copies, waits for them, and re-layouts  1.89 us (3%)
    pallas_call x1, Pallas kernels, local(): pl.pallas_call(kernel, out_shape=jax.ShapeDtypeStruct((ROWS, 4, 2, 16, CH...  65 us
    unnamed x1, local copies, waits for them, and re-layouts  1.89 us

profile of v2, /device:TPU:0, one launch (start us, length us, event | category | flops | bytes accessed | tf_op | source)
XLA Modules:
  0.0 67.5 jit_solution(14960669057757262672)
XLA Ops:
  0.7 65.0 %triangle.1 = bf16[16,4,2,16,128]{4,3,2,1,0:T(8,128)(2,1)} custom-call(s32[1]{0:T(128)S(6)} %copy.11.count_ref, bf16[16,128,128]{2,1,0:T(8,128)(2,1)} %pa_in.1, bf16[128,256]{1,0:T(8,128)(2,1)} %ep_in.1, bf16[128,256]{1,0:T(8,128)(2,1)} %eg_in.1, bf16[128,128]{1,0:T(8,128)(2,1)} %tg_in.1, bf16[128,128]{1,0:T(8,128)(2,1)} %to_in.1, bf16[128,512]{1,0:T(8,128)(2,1)} %ap_in.1, ...), custom_call_target="tpu_custom_call" | custom-call | tf_op jit(solution)/shard_map/triangle/pallas_call | solution.py:389
  65.6 1.9 %copy.12 = bf16[16,128,128]{2,1,0:T(8,128)(2,1)} copy(bf16[16,128,128]{2,1,0:T(8,128)(2,1)} %bitcast.2) | data formatting | bytes 1048576

commit v3 on v2

--- a/solution.py
+++ b/solution.py
@@ -58,7 +58,7 @@
     out,
     pa, ep, eg, tg, to, ap, bp, ao, wt, nrm, ebuf, esend, lr, tst, tsend, trecv, tn, gbuf, a2, upd, an, qs, ks, vs, gs, ba, bb, bc, sbuf, bias, osend,
     ready, load, pa_send, pa_recv, pa_own, e_send, e_recv, t_send, t_recv,
-    b_send, b_recv, u_send, u_recv, o_send, o_recv,
+    p_send, p_recv, l_send, l_recv, u_send, u_recv, o_send, o_recv,
 ):
     r = lax.axis_index("row")
     q = lax.axis_index("ch")
@@ -154,10 +154,10 @@
             if (offset[0] + offset[1] + offset[3]) % 4 == k:
                 rr, qq = peer(offset)
                 rows = pl.ds(pl.multiple_of(rr * 32, 32), 32)
-                remote(esend.at[k, rows], lr.at[q, r], e_send, e_recv, rr, qq).start()
+                remote(esend.at[k, rows], lr.at[q, z * LINE + y, core], e_send, e_recv, rr, qq).start()
 
     own = pl.ds(pl.multiple_of(r * 32, 32), 32)
-    pltpu.make_async_copy(esend.at[0, own], lr.at[q, r], e_recv).start()
+    pltpu.make_async_copy(esend.at[0, own], lr.at[q, z * LINE + y, core], e_recv).start()
 
     pa_copies = []
     for dq in range(1, LINE):
@@ -171,37 +171,32 @@
     pa_local.start()
 
     settle(lr, e_recv)
-    right = jnp.concatenate([lr[k, :, 16:32, :].reshape(TOK, COLS) for k in range(LINE)], axis=1)
-    for half in range(2):
+    right = jnp.concatenate([lr[k, :, :, 16:32, :].reshape(TOK, COLS) for k in range(LINE)], axis=1)
+    for dc in (1, 0):
         left = jnp.concatenate(
-            [lr[k, half * 16 : half * 16 + 16, 0:16, :].reshape(256, COLS) for k in range(LINE)],
-            axis=1,
+            [lr[k, :, cores[dc], 0:16, :].reshape(256, COLS) for k in range(LINE)], axis=1
         )
         tri = dot(left, right, NT)
         for jb in range(LINE):
-            tst[pl.ds(half * 1024 + jb, 256, stride=4), :] = tri[:, jb * 128 : jb * 128 + 128]
-
-    @pl.loop(0, 4)
-    def _(part):
-        rows = pl.ds(pl.multiple_of(part * 512, 512), 512)
-        tsend[rows, :] = tst[rows, :].astype(BF16)
-
-    for offset in FAR_FIRST:
-        rr, qq = peer(offset)
-        rows = pl.ds(pl.multiple_of((rr * LINE + qq) * 16, 16), 16)
-        remote(tsend.at[rows], trecv.at[me], t_send, t_recv, rr, qq).start()
-
-    own = pl.ds(pl.multiple_of(me * 16, 16), 16)
-    pltpu.make_async_copy(tsend.at[own], trecv.at[me], t_recv).start()
+            tst[dc, pl.ds(jb, 256, stride=4), :] = tri[:, jb * 128 : jb * 128 + 128]
+        tsend[dc] = tst[dc].astype(BF16)
+        for offset in FAR_FIRST:
+            if offset[2] == dc:
+                rr, qq = peer(offset)
+                rows = pl.ds(pl.multiple_of((zs[offset[0]] * 16 + ys[offset[1]] * 4 + qq) * 16, 16), 16)
+                remote(tsend.at[dc, rows], trecv.at[me], t_send, t_recv, rr, qq).start()
+
+    own = pl.ds(pl.multiple_of((z * 16 + y * 4 + q) * 16, 16), 16)
+    pltpu.make_async_copy(tsend.at[0, own], trecv.at[me], t_recv).start()
 
     pa_local.wait()
     for copy in pa_copies:
         copy.wait()
 
     @pl.loop(0, OWN)
-    def _(il):
-        x = a2[:, il].reshape(TOK, CH).astype(F32)
-        gbuf[il] = sigmoid(dot(layer_norm(x).astype(BF16), tg[...]))
+    def _(jb):
+        x = a2[jb].reshape(TOK, CH).astype(F32)
+        gbuf[jb] = sigmoid(dot(layer_norm(x).astype(BF16), tg[...]))
 
     settle(trecv, t_recv)
 
@@ -226,54 +221,64 @@
     spot = lax.broadcasted_iota(jnp.int32, (16, HEADS), 0) % HEADS
     pick = (spot == lax.broadcasted_iota(jnp.int32, (16, HEADS), 1)).astype(BF16)
     bias_w = dot(pick, bp[...]).astype(BF16)
-    bias_row = lax.broadcasted_iota(jnp.int32, (16, TOK), 0) // HEADS
-
-    def update(il, own_bias):
+    bias_row = lax.broadcasted_iota(jnp.int32, (16, 128), 0) // HEADS
+
+    u = z + core * (y - z)
+    v = y + core * (z - y)
+    us = [lax.rem(u + d, LINE) for d in range(LINE)]
+    vvs = [lax.rem(v + d, LINE) for d in range(LINE)]
+    step_u = 8 - 6 * core
+    step_v = 2 + 6 * core
+    parts = [(ba, us, vvs, xs), (bb, vvs, us, xs), (bc, xs, us, vvs)]
+
+    def at(n, line, first, second):
+        uu, vv, xx = [
+            (us[line], vvs[first], xs[second]),
+            (us[first], vvs[line], xs[second]),
+            (us[first], vvs[second], xs[line]),
+        ][n]
+        return uu * step_u + vv * step_v + core, xx
+
+    def over_plane(n):
+        ref, lines, firsts, seconds = parts[n]
+        slot = ref.at[lines[0], firsts[0] * LINE + seconds[0]]
+        pairs = [(f, t) for f in range(LINE) for t in range(LINE)][1:]
+        for f, t in sorted(pairs, key=lambda p: -min(p[0], LINE - p[0]) - min(p[1], LINE - p[1])):
+            remote(slot, slot, p_send.at[n], p_recv.at[n], *at(n, 0, f, t)).start()
+
+    def along_line(n):
+        ref, lines, _, _ = parts[n]
+        settle(ref.at[lines[0], 0:15], p_recv.at[n])
+        for d in (2, 1, 3):
+            slot = ref.at[lines[0]]
+            remote(slot, slot, l_send.at[n], l_recv.at[n], *at(n, d, 0, 0)).start()
+
+    mine = pl.ds(core * OWN, OWN)
+    for jb in range(LINE):
         blocks = [
-            tn[pl.ds(il * LINE + jb, 128, stride=20), :].T.astype(BF16) for jb in range(LINE)
+            tn[pl.ds(il * LINE + jb, 128, stride=20), :].T.astype(BF16) for il in range(OWN)
         ]
         product = dot(jnp.concatenate(blocks, axis=0), to[...])
-        x = a2[:, il].reshape(TOK, CH).astype(F32)
-        updated = (x + gbuf[il] * product).astype(BF16)
-        upd[core * OWN + il] = updated.reshape(16, 2, 16, CH)
+        x = a2[jb].reshape(TOK, CH).astype(F32)
+        updated = (x + gbuf[jb] * product).astype(BF16)
+        upd[mine, jb * 4 : jb * 4 + 4] = updated.reshape(OWN, 4, 2, 16, CH)
         normed = layer_norm(updated.astype(F32)).astype(BF16)
-        an[il] = normed.reshape(16, 2, 16, CH)
-        return jnp.where(bias_row == il, dot(bias_w, normed, NT), own_bias)
-
-    own_bias = lax.fori_loop(0, OWN, update, jnp.zeros((16, TOK), F32)).astype(BF16)
-    ba[z, y, q, 0:16, :] = own_bias[:, 0:128]
-    ba[z, y, q, 16:32, :] = own_bias[:, 128:256]
-    bb[y, q, z] = own_bias[:, 256:384]
-    bc[q, z, y] = own_bias[:, 384:512]
-
-    parts = [(ba, "zyx"), (bb, "yxz"), (bc, "xzy")]
-    at = {"z": zs, "y": ys, "x": xs}
-
-    def spread(stage):
-        copies = []
-        for n, (ref, axes) in enumerate(parts):
-            slot = ref.at[tuple(at[axis][0] for axis in axes[: 3 - stage])]
-            for d in range(1, LINE):
-                offset = {"z": 0, "y": 0, "x": 0}
-                offset[axes[2 - stage]] = d
-                rr, qq = peer((offset["z"], offset["y"], 0, offset["x"]))
-                sem = stage * 9 + n * 3 + d - 1
-                copies.append(remote(slot, slot, b_send.at[sem], b_recv.at[sem], rr, qq))
-        for copy in copies:
-            copy.start()
-        return copies
-
-    def spread_wait(stage):
-        for n, (ref, axes) in enumerate(parts):
-            for d in range(1, LINE):
-                place_of = [at[axis][0] for axis in axes[: 3 - stage]]
-                place_of[-1] = at[axes[2 - stage]][LINE - d]
-                settle(ref.at[tuple(place_of)], b_recv.at[stage * 9 + n * 3 + d - 1])
-
-    copies = spread(0)
+        an[:, jb * 4 : jb * 4 + 4] = normed.reshape(OWN, 4, 2, 16, CH)
+        biases = dot(bias_w, normed, NT)
+        tile = biases[:, 0:128]
+        for il in range(1, OWN):
+            tile = jnp.where(bias_row == il, biases[:, il * 128 : il * 128 + 128], tile)
+        tile = tile.astype(BF16)
+        if jb < 2:
+            ba[u, v * LINE + q, jb * 16 : jb * 16 + 16, :] = tile
+        elif jb == 2:
+            bb[v, u * LINE + q] = tile
+        else:
+            bc[q, u * LINE + v] = tile
+        if jb > 0:
+            over_plane(jb - 1)
+
     twin = place(z, y, 1 - core)
-    mine = pl.ds(core * OWN, OWN)
-    theirs = pl.ds((1 - core) * OWN, OWN)
     swap = remote(upd.at[mine], upd.at[mine], u_send, u_recv, twin, q)
     swap.start()
 
@@ -301,15 +306,15 @@
         project(il, il)
 
     score(0)
-    spread_wait(0)
-    copies += spread(1)
-
-    @pl.loop(1, OWN)
+    along_line(0)
+    score(1)
+    along_line(1)
+    along_line(2)
+
+    @pl.loop(2, OWN)
     def _(n):
         score(n)
 
-    spread_wait(1)
-    copies += spread(2)
     swap.wait_recv()
 
     @pl.loop(0, OWN)
@@ -322,21 +327,26 @@
     def _(n):
         score(n)
 
-    spread_wait(2)
+    for n, (ref, _, _, _) in enumerate(parts):
+        settle(ref.at[0:3], l_recv.at[n])
     key_lane = lax.broadcasted_iota(jnp.int32, (1, TOK), 1)
     key_term = jnp.where(key_lane < count, 0.0, -1e9 * LOG2E)
+    rows_u = 256 - 192 * core
+    rows_v = 64 + 192 * core
 
     @pl.loop(0, LINE)
-    def _(zz):
-        for yy in range(LINE):
+    def _(uu):
+        for vv in range(LINE):
             for xx in range(LINE):
-                rows = pl.ds(pl.multiple_of(zz * 256 + yy * 64 + xx * 16, 16), 16)
-                tiles = [ba[zz, yy, xx, 0:16], ba[zz, yy, xx, 16:32], bb[yy, xx, zz], bc[xx, zz, yy]]
+                rows = pl.ds(pl.multiple_of(uu * rows_u + vv * rows_v + xx * 16, 16), 16)
+                pair = ba[uu, vv * LINE + xx]
+                tiles = [pair[0:16], pair[16:32], bb[vv, uu * LINE + xx], bc[xx, uu * LINE + vv]]
                 for kb, tile in enumerate(tiles):
                     cols = slice(kb * 128, kb * 128 + 128)
                     bias[kb, rows, :] = tile.astype(F32) * LOG2E + key_term[:, cols]
 
-    def attend(n, own_row):
+    @pl.loop(0, 2 * OWN)
+    def _(n):
         weights = []
         for h in range(HEADS):
             for part in range(4):
@@ -352,35 +362,28 @@
             total = jnp.where(mask, mixed[h * 256 : h * 256 + 256], total)
         attended = total[:, 0:CH] / total[:, CH : 2 * CH]
         gated = (attended * gs[n]).astype(BF16)
-        before = upd[own_row, :, core].reshape(256, CH).astype(F32)
+        owner = core + (1 - 2 * core) * (n // OWN)
+        before = upd[owner * OWN + n % OWN, :, core].reshape(256, CH).astype(F32)
         result = before + dot(gated, ao[...])
         osend[n] = result.astype(BF16).reshape(LINE, 4, 16, CH)
-
-    @pl.loop(0, OWN)
-    def _(il):
-        attend(OWN + il, (1 - core) * OWN + il)
-        for d in range(LINE):
-            jb = xs[d]
-            target = out.at[q * OWN + il, :, core]
-            remote(osend.at[OWN + il, jb], target, o_send, o_recv, twin, jb).start()
-
-    @pl.loop(0, OWN)
-    def _(il):
-        attend(il, core * OWN + il)
-        target = out.at[q * OWN + il, :, core]
-        for d in range(1, LINE):
-            jb = xs[d]
-            remote(osend.at[il, jb], target, o_send, o_recv, r, jb).start()
-        pltpu.make_async_copy(osend.at[il, q], target, o_recv).start()
+        target = out.at[q * OWN + n % OWN, :, core]
+        for d in (2, 1, 3):
+            remote(osend.at[n, xs[d]], target, o_send, o_recv, place(z, y, owner), xs[d]).start()
+
+    target = out.at[pl.ds(q * OWN, OWN), :, core]
+    remote(osend.at[OWN : 2 * OWN, q], target, o_send, o_recv, twin, q).start()
+    pltpu.make_async_copy(osend.at[0:OWN, q], target, o_recv).start()
 
     settle(out, o_recv)
     settle(osend.at[0:7], o_send)
     settle(esend.at[0:3], e_send)
     settle(esend.at[0, 0 : 31 * 32], e_send)
-    settle(tsend.at[0 : 16 * (DEVICES - 1)], t_send)
+    settle(tsend.at[1], t_send)
+    settle(tsend.at[0, 0 : 63 * 16], t_send)
     swap.wait_send()
-    for copy in copies:
-        copy.wait_send()
+    for n, (ref, _, _, _) in enumerate(parts):
+        settle(ref.at[0, 0:15], p_send.at[n])
+        settle(ref.at[0:3], l_send.at[n])
 
 
 def local(pair_act, valid_count, edge_proj, edge_gate, tri_gate, tri_out, attn_proj, bias_proj, attn_out):
@@ -404,9 +407,9 @@
             pltpu.VMEM((2048, CH), BF16),
             pltpu.VMEM((32 * 36, COLS), F32),
             pltpu.VMEM((4, 1024, COLS), BF16),
-            pltpu.VMEM((LINE, 32, 32, COLS), BF16),
-            pltpu.VMEM((2048, 128), F32),
-            pltpu.VMEM((2048, 128), BF16),
+            pltpu.VMEM((LINE, 16, 2, 32, COLS), BF16),
+            pltpu.VMEM((2, 1024, 128), F32),
+            pltpu.VMEM((2, 1024, 128), BF16),
             pltpu.VMEM((CH, 16, 128), BF16),
             pltpu.VMEM((CH * 20, 128), F32),
             pltpu.VMEM((OWN, TOK, CH), F32),
@@ -417,14 +420,14 @@
             pltpu.VMEM((2 * OWN, TOK, CH), BF16),
             pltpu.VMEM((2 * OWN, TOK, 2 * CH), BF16),
             pltpu.VMEM((2 * OWN, 256, CH), F32),
-            pltpu.VMEM((LINE, LINE, LINE, 32, 128), BF16),
-            pltpu.VMEM((LINE, LINE, LINE, 16, 128), BF16),
-            pltpu.VMEM((LINE, LINE, LINE, 16, 128), BF16),
+            pltpu.VMEM((LINE, 16, 32, 128), BF16),
+            pltpu.VMEM((LINE, 16, 16, 128), BF16),
+            pltpu.VMEM((LINE, 16, 16, 128), BF16),
             pltpu.VMEM((2 * OWN, 1024, TOK), F32),
             pltpu.VMEM((LINE, 1024, 128), F32),
             pltpu.VMEM((2 * OWN, LINE, 4, 16, CH), BF16),
             pltpu.SemaphoreType.REGULAR, dma((8,)), dma((3,)), dma((3,)), dma, dma, dma, dma, dma,
-            dma((27,)), dma((27,)), dma, dma, dma, dma,
+            dma((3,)), dma((3,)), dma((3,)), dma((3,)), dma, dma, dma, dma,
         ],
         compiler_params=pltpu.CompilerParams(
             collective_id=0, has_side_effects=True, vmem_limit_bytes=63 * 1024 * 1024

time: 67.7 us -> 63.1 us (0.932)
  the two profiles are of different devices: /device:TPU:0 before, /device:TPU:1 now
where the time goes in v3:
time: 63.1 us; the launch traced here: 62.9 us
  Pallas kernels  60.4 us (96%)
  local copies, waits for them, and re-layouts  1.89 us (3%)
  between operations  0.66 us (1%)
    pallas_call x1, Pallas kernels, local(): pl.pallas_call(kernel, out_shape=jax.ShapeDtypeStruct((ROWS, 4, 2, 16, CH...  60.4 us
    unnamed x1, local copies, waits for them, and re-layouts  1.89 us

profile of v3, /device:TPU:1, one launch (start us, length us, event | category | flops | bytes accessed | tf_op | source)
XLA Modules:
  0.0 62.9 jit_solution(15797218945427556096)
XLA Ops:
  0.7 60.4 %triangle.1 = bf16[16,4,2,16,128]{4,3,2,1,0:T(8,128)(2,1)} custom-call(s32[1]{0:T(128)S(6)} %copy.11.count_ref, bf16[16,128,128]{2,1,0:T(8,128)(2,1)} %pa_in.1, bf16[128,256]{1,0:T(8,128)(2,1)} %ep_in.1, bf16[128,256]{1,0:T(8,128)(2,1)} %eg_in.1, bf16[128,128]{1,0:T(8,128)(2,1)} %tg_in.1, bf16[128,128]{1,0:T(8,128)(2,1)} %to_in.1, bf16[128,512]{1,0:T(8,128)(2,1)} %ap_in.1, ...), custom_call_target="tpu_custom_call" | custom-call | tf_op jit(solution)/shard_map/triangle/pallas_call | solution.py:392
  61.0 1.9 %copy.12 = bf16[16,128,128]{2,1,0:T(8,128)(2,1)} copy(bf16[16,128,128]{2,1,0:T(8,128)(2,1)} %bitcast.2) | data formatting | bytes 1048576

commit v4 on v3

--- a/solution.py
+++ b/solution.py
@@ -56,7 +56,7 @@
 def kernel(
     count_ref, pa_in, ep_in, eg_in, tg_in, to_in, ap_in, bp_in, ao_in,
     out,
-    pa, ep, eg, tg, to, ap, bp, ao, wt, nrm, ebuf, esend, lr, tst, tsend, trecv, tn, gbuf, a2, upd, an, qs, ks, vs, gs, ba, bb, bc, sbuf, bias, osend,
+    pa, ep, eg, tg, to, ap, bp, ao, wt, nrm, ebuf, esend, lr, tst, tsend, trecv, tn, gbuf, a2, upd, an, qs, ks, vs, gs, ba, bb, bc, sbuf, raw, bias, osend,
     ready, load, pa_send, pa_recv, pa_own, e_send, e_recv, t_send, t_recv,
     p_send, p_recv, l_send, l_recv, u_send, u_recv, o_send, o_recv,
 ):
@@ -150,14 +150,44 @@
         edges_of(k)
         if step == 0:
             pl.semaphore_wait(ready, len(plane))
-        for offset in FAR_FIRST:
-            if (offset[0] + offset[1] + offset[3]) % 4 == k:
+        targets = [o for o in FAR_FIRST if (o[0] + o[1] + o[3]) % 4 == k]
+
+        @pl.when(core == 0)
+        def _():
+            for offset in targets:
                 rr, qq = peer(offset)
                 rows = pl.ds(pl.multiple_of(rr * 32, 32), 32)
-                remote(esend.at[k, rows], lr.at[q, z * LINE + y, core], e_send, e_recv, rr, qq).start()
-
-    own = pl.ds(pl.multiple_of(r * 32, 32), 32)
-    pltpu.make_async_copy(esend.at[0, own], lr.at[q, z * LINE + y, core], e_recv).start()
+                remote(esend.at[k, rows], lr.at[q, z * LINE + y, 0], e_send.at[0], e_recv.at[0], rr, qq).start()
+
+        @pl.when(core == 1)
+        def _():
+            for offset in targets:
+                rr, qq = peer(offset)
+                rows = pl.ds(pl.multiple_of(rr * 32 + 16, 16), 16)
+                remote(
+                    esend.at[k, rows], lr.at[q, z * LINE + y, 1, 16:32], e_send.at[1], e_recv.at[1], rr, qq
+                ).start()
+
+    @pl.when(core == 0)
+    def _():
+        own = pl.ds(pl.multiple_of(r * 32, 32), 32)
+        pltpu.make_async_copy(esend.at[0, own], lr.at[q, z * LINE + y, 0], e_recv.at[0]).start()
+
+    @pl.when(core == 1)
+    def _():
+        own = pl.ds(pl.multiple_of(r * 32 + 16, 16), 16)
+        pltpu.make_async_copy(esend.at[0, own], lr.at[q, z * LINE + y, 1, 16:32], e_recv.at[1]).start()
+        settle(tsend.at[0], e_send.at[1])
+        settle(tsend.at[0, 0 : 63 * 16], e_send.at[1])
+        for offset in FAR_FIRST:
+            rr, qq = peer(offset)
+            rows = pl.ds(pl.multiple_of(rr * 32, 32), 16)
+            k = (offset[0] + offset[1] + offset[3]) % 4
+            remote(
+                esend.at[k, rows], lr.at[q, z * LINE + y, 1, 0:16], e_send.at[2], e_recv.at[2], rr, qq
+            ).start()
+        own = pl.ds(pl.multiple_of(r * 32, 32), 16)
+        pltpu.make_async_copy(esend.at[0, own], lr.at[q, z * LINE + y, 1, 0:16], e_recv.at[2]).start()
 
     pa_copies = []
     for dq in range(1, LINE):
@@ -170,24 +200,37 @@
     pa_local = pltpu.make_async_copy(pa.at[pl.ds(q * OWN, OWN)], a2.at[q], pa_own)
     pa_local.start()
 
-    settle(lr, e_recv)
+    settle(lr.at[:, :, 0], e_recv.at[0])
+    settle(lr.at[:, :, 1, 16:32], e_recv.at[1])
     right = jnp.concatenate([lr[k, :, :, 16:32, :].reshape(TOK, COLS) for k in range(LINE)], axis=1)
-    for dc in (1, 0):
+    for half in range(2):
+        if half == 1:
+            settle(lr.at[:, :, 1, 0:16], e_recv.at[2])
         left = jnp.concatenate(
-            [lr[k, :, cores[dc], 0:16, :].reshape(256, COLS) for k in range(LINE)], axis=1
+            [lr[k, :, half, 0:16, :].reshape(256, COLS) for k in range(LINE)], axis=1
         )
         tri = dot(left, right, NT)
         for jb in range(LINE):
-            tst[dc, pl.ds(jb, 256, stride=4), :] = tri[:, jb * 128 : jb * 128 + 128]
-        tsend[dc] = tst[dc].astype(BF16)
+            tst[half, pl.ds(jb, 256, stride=4), :] = tri[:, jb * 128 : jb * 128 + 128]
+        tsend[half] = tst[half].astype(BF16)
         for offset in FAR_FIRST:
-            if offset[2] == dc:
-                rr, qq = peer(offset)
-                rows = pl.ds(pl.multiple_of((zs[offset[0]] * 16 + ys[offset[1]] * 4 + qq) * 16, 16), 16)
-                remote(tsend.at[dc, rows], trecv.at[me], t_send, t_recv, rr, qq).start()
-
-    own = pl.ds(pl.multiple_of((z * 16 + y * 4 + q) * 16, 16), 16)
-    pltpu.make_async_copy(tsend.at[0, own], trecv.at[me], t_recv).start()
+            if offset[2] == 0:
+                zz, yy, qq = zs[offset[0]], ys[offset[1]], xs[offset[3]]
+                rows = pl.ds(pl.multiple_of((zz * 16 + yy * 4 + qq) * 16, 16), 16)
+                remote(
+                    tsend.at[half, rows], trecv.at[me], t_send.at[half], t_recv, place(zz, yy, half), qq
+                ).start()
+        own = pl.ds(pl.multiple_of((z * 16 + y * 4 + q) * 16, 16), 16)
+
+        @pl.when(core == half)
+        def _():
+            pltpu.make_async_copy(tsend.at[half, own], trecv.at[me], t_recv).start()
+
+        @pl.when(core != half)
+        def _():
+            remote(
+                tsend.at[half, own], trecv.at[me], t_send.at[half], t_recv, place(z, y, half), q
+            ).start()
 
     pa_local.wait()
     for copy in pa_copies:
@@ -275,8 +318,10 @@
             bb[v, u * LINE + q] = tile
         else:
             bc[q, u * LINE + v] = tile
-        if jb > 0:
-            over_plane(jb - 1)
+        if jb == 1:
+            over_plane(0)
+    over_plane(1)
+    over_plane(2)
 
     twin = place(z, y, 1 - core)
     swap = remote(upd.at[mine], upd.at[mine], u_send, u_recv, twin, q)
@@ -343,16 +388,18 @@
                 tiles = [pair[0:16], pair[16:32], bb[vv, uu * LINE + xx], bc[xx, uu * LINE + vv]]
                 for kb, tile in enumerate(tiles):
                     cols = slice(kb * 128, kb * 128 + 128)
-                    bias[kb, rows, :] = tile.astype(F32) * LOG2E + key_term[:, cols]
-
-    @pl.loop(0, 2 * OWN)
-    def _(n):
+                    raw[kb, rows, :] = tile.astype(F32) * LOG2E + key_term[:, cols]
+
+    for kb in range(LINE):
+        for h in range(HEADS):
+            bias[h, :, kb * 128 : kb * 128 + 128] = raw[kb, pl.ds(h, 256, stride=4), :]
+
+    def attend(n, owner):
         weights = []
         for h in range(HEADS):
             for part in range(4):
                 rows = slice(h * 256 + part * 64, h * 256 + part * 64 + 64)
-                own = [bias[kb, pl.ds(part * 256 + h, 64, stride=4), :] for kb in range(LINE)]
-                logits = sbuf[n, rows, :] + jnp.concatenate(own, axis=1)
+                logits = sbuf[n, rows, :] + bias[h, part * 64 : part * 64 + 64, :]
                 powers = jnp.exp2(logits - jnp.max(logits, axis=-1, keepdims=True))
                 weights.append(powers.astype(BF16))
         mixed = dot(jnp.concatenate(weights, axis=0), vs[n])
@@ -362,7 +409,6 @@
             total = jnp.where(mask, mixed[h * 256 : h * 256 + 256], total)
         attended = total[:, 0:CH] / total[:, CH : 2 * CH]
         gated = (attended * gs[n]).astype(BF16)
-        owner = core + (1 - 2 * core) * (n // OWN)
         before = upd[owner * OWN + n % OWN, :, core].reshape(256, CH).astype(F32)
         result = before + dot(gated, ao[...])
         osend[n] = result.astype(BF16).reshape(LINE, 4, 16, CH)
@@ -370,16 +416,36 @@
         for d in (2, 1, 3):
             remote(osend.at[n, xs[d]], target, o_send, o_recv, place(z, y, owner), xs[d]).start()
 
+    @pl.loop(OWN, 2 * OWN)
+    def _(n):
+        attend(n, 1 - core)
+
     target = out.at[pl.ds(q * OWN, OWN), :, core]
     remote(osend.at[OWN : 2 * OWN, q], target, o_send, o_recv, twin, q).start()
+
+    @pl.loop(0, OWN)
+    def _(n):
+        attend(n, core)
+
     pltpu.make_async_copy(osend.at[0:OWN, q], target, o_recv).start()
 
     settle(out, o_recv)
     settle(osend.at[0:7], o_send)
-    settle(esend.at[0:3], e_send)
-    settle(esend.at[0, 0 : 31 * 32], e_send)
-    settle(tsend.at[1], t_send)
-    settle(tsend.at[0, 0 : 63 * 16], t_send)
+
+    @pl.when(core == 0)
+    def _():
+        settle(esend.at[0:3], e_send.at[0])
+        settle(esend.at[0, 0 : 31 * 32], e_send.at[0])
+        settle(tsend.at[0, 0 : 63 * 16], t_send.at[0])
+        settle(tsend.at[1], t_send.at[1])
+
+    @pl.when(core == 1)
+    def _():
+        settle(tsend.at[0], e_send.at[2])
+        settle(tsend.at[0, 0 : 63 * 16], e_send.at[2])
+        settle(tsend.at[0], t_send.at[0])
+        settle(tsend.at[1, 0 : 63 * 16], t_send.at[1])
+
     swap.wait_send()
     for n, (ref, _, _, _) in enumerate(parts):
         settle(ref.at[0, 0:15], p_send.at[n])
@@ -425,8 +491,9 @@
             pltpu.VMEM((LINE, 16, 16, 128), BF16),
             pltpu.VMEM((2 * OWN, 1024, TOK), F32),
             pltpu.VMEM((LINE, 1024, 128), F32),
+            pltpu.VMEM((HEADS, 256, TOK), F32),
             pltpu.VMEM((2 * OWN, LINE, 4, 16, CH), BF16),
-            pltpu.SemaphoreType.REGULAR, dma((8,)), dma((3,)), dma((3,)), dma, dma, dma, dma, dma,
+            pltpu.SemaphoreType.REGULAR, dma((8,)), dma((3,)), dma((3,)), dma, dma((3,)), dma((3,)), dma((2,)), dma,
             dma((3,)), dma((3,)), dma((3,)), dma((3,)), dma, dma, dma, dma,
         ],
         compiler_params=pltpu.CompilerParams(

time: 63.1 us -> 60.8 us (0.964)
  Pallas kernels: 60.4 us -> 58 us
    pallas_call x1, Pallas kernels: 60.4 us -> 58 us  [local(): pl.pallas_call(kernel, out_shape=jax.ShapeDtypeStruct((ROWS, 4, 2, 16, CH...]
where the time goes in v4:
time: 60.8 us; the launch traced here: 60.6 us
  Pallas kernels  58 us (95%)
  local copies, waits for them, and re-layouts  1.89 us (3%)
  between operations  0.66 us (1%)
    pallas_call x1, Pallas kernels, local(): pl.pallas_call(kernel, out_shape=jax.ShapeDtypeStruct((ROWS, 4, 2, 16, CH...  58 us
    unnamed x1, local copies, waits for them, and re-layouts  1.89 us

profile of v4, /device:TPU:1, one launch (start us, length us, event | category | flops | bytes accessed | tf_op | source)
XLA Modules:
  0.0 60.6 jit_solution(9999728577019491211)
XLA Ops:
  0.7 58.0 %triangle.1 = bf16[16,4,2,16,128]{4,3,2,1,0:T(8,128)(2,1)} custom-call(s32[1]{0:T(128)S(6)} %copy.11.count_ref, bf16[16,128,128]{2,1,0:T(8,128)(2,1)} %pa_in.1, bf16[128,256]{1,0:T(8,128)(2,1)} %ep_in.1, bf16[128,256]{1,0:T(8,128)(2,1)} %eg_in.1, bf16[128,128]{1,0:T(8,128)(2,1)} %tg_in.1, bf16[128,128]{1,0:T(8,128)(2,1)} %to_in.1, bf16[128,512]{1,0:T(8,128)(2,1)} %ap_in.1, ...), custom_call_target="tpu_custom_call" | custom-call | tf_op jit(solution)/shard_map/triangle/pallas_call | solution.py:458
  58.7 1.9 %copy.12 = bf16[16,128,128]{2,1,0:T(8,128)(2,1)} copy(bf16[16,128,128]{2,1,0:T(8,128)(2,1)} %bitcast.2) | data formatting | bytes 1048576

commit v5 on v4

--- a/solution.py
+++ b/solution.py
@@ -54,9 +54,9 @@
 
 
 def kernel(
-    count_ref, pa_in, ep_in, eg_in, tg_in, to_in, ap_in, bp_in, ao_in,
+    count_in, pa_in, ep_in, eg_in, tg_in, to_in, ap_in, bp_in, ao_in,
     out,
-    pa, ep, eg, tg, to, ap, bp, ao, wt, nrm, ebuf, esend, lr, tst, tsend, trecv, tn, gbuf, a2, upd, an, qs, ks, vs, gs, ba, bb, bc, sbuf, raw, bias, osend,
+    count, pa, ep, eg, tg, to, ap, bp, ao, wt, nrm, ebuf, esend, lr, tst, tsend, trecv, tn, gbuf, a2, upd, an, qs, ks, vs, gs, ba, bb, bc, sbuf, raw, bias, osend,
     ready, load, pa_send, pa_recv, pa_own, e_send, e_recv, t_send, t_recv,
     p_send, p_recv, l_send, l_recv, u_send, u_recv, o_send, o_recv,
 ):
@@ -66,7 +66,6 @@
     z = lax.div(r, 8)
     y = lax.rem(lax.div(r, 2), 4)
     core = lax.rem(r, 2)
-    count = count_ref[0]
 
     def place(zz, yy, cc):
         return zz * 8 + yy * 2 + cc
@@ -92,7 +91,7 @@
     loads = [
         pltpu.make_async_copy(src, dst, load.at[n])
         for n, (src, dst) in enumerate(
-            [(ep_in, ep), (eg_in, eg), (pa_in, pa), (tg_in, tg), (to_in, to), (ap_in, ap), (bp_in, bp), (ao_in, ao)]
+            [(count_in, count), (ep_in, ep), (eg_in, eg), (pa_in, pa), (tg_in, tg), (to_in, to), (ap_in, ap), (bp_in, bp), (ao_in, ao)]
         )
     ]
     for copy in loads:
@@ -136,7 +135,7 @@
             both = dot(weights, nrm[part * 512 : part * 512 + 512, :], NT)
             row_token = r * ROWS + part * 4 + lane // 128
             col_token = q * COLS + lane % 128
-            valid = jnp.where((row_token < count) & (col_token < count), 1.0, 0.0)
+            valid = jnp.where((row_token < count[...]) & (col_token < count[...]), 1.0, 0.0)
             edges = sigmoid(both[64:128]) * both[0:64] * valid
             for i in range(4):
                 for side in range(2):
@@ -287,13 +286,14 @@
         slot = ref.at[lines[0], firsts[0] * LINE + seconds[0]]
         pairs = [(f, t) for f in range(LINE) for t in range(LINE)][1:]
         for f, t in sorted(pairs, key=lambda p: -min(p[0], LINE - p[0]) - min(p[1], LINE - p[1])):
-            remote(slot, slot, p_send.at[n], p_recv.at[n], *at(n, 0, f, t)).start()
-
-    def along_line(n):
-        ref, lines, _, _ = parts[n]
-        settle(ref.at[lines[0], 0:15], p_recv.at[n])
+            remote(slot, slot, p_send.at[n], p_recv.at[n * LINE + f], *at(n, 0, f, t)).start()
+
+    def along_line(n, f):
+        ref, lines, firsts, _ = parts[n]
+        settle(ref.at[lines[0], 0 : 3 if f == 0 else 4], p_recv.at[n * LINE + f])
+        entries = pl.ds(firsts[(LINE - f) % LINE] * LINE, LINE)
         for d in (2, 1, 3):
-            slot = ref.at[lines[0]]
+            slot = ref.at[lines[0], entries]
             remote(slot, slot, l_send.at[n], l_recv.at[n], *at(n, d, 0, 0)).start()
 
     mine = pl.ds(core * OWN, OWN)
@@ -350,11 +350,15 @@
     def _(il):
         project(il, il)
 
+    for f in (0, 1):
+        for n in range(3):
+            along_line(n, f)
     score(0)
-    along_line(0)
+    for n in range(3):
+        along_line(n, 3)
     score(1)
-    along_line(1)
-    along_line(2)
+    for n in range(3):
+        along_line(n, 2)
 
     @pl.loop(2, OWN)
     def _(n):
@@ -375,7 +379,7 @@
     for n, (ref, _, _, _) in enumerate(parts):
         settle(ref.at[0:3], l_recv.at[n])
     key_lane = lax.broadcasted_iota(jnp.int32, (1, TOK), 1)
-    key_term = jnp.where(key_lane < count, 0.0, -1e9 * LOG2E)
+    key_term = jnp.where(key_lane < count[...], 0.0, -1e9 * LOG2E)
     rows_u = 256 - 192 * core
     rows_v = 64 + 192 * core
 
@@ -458,9 +462,10 @@
     return pl.pallas_call(
         kernel,
         out_shape=jax.ShapeDtypeStruct((ROWS, 4, 2, 16, CH), BF16),
-        in_specs=[pl.BlockSpec(memory_space=pltpu.SMEM)] + [hbm] * 8,
+        in_specs=[hbm] * 9,
         out_specs=pl.BlockSpec(memory_space=pl.ANY),
         scratch_shapes=[
+            pltpu.VMEM((1, 1), jnp.int32),
             pltpu.VMEM((ROWS, COLS, CH), BF16),
             pltpu.VMEM((CH, 2 * CH), BF16),
             pltpu.VMEM((CH, 2 * CH), BF16),
@@ -493,14 +498,14 @@
             pltpu.VMEM((LINE, 1024, 128), F32),
             pltpu.VMEM((HEADS, 256, TOK), F32),
             pltpu.VMEM((2 * OWN, LINE, 4, 16, CH), BF16),
-            pltpu.SemaphoreType.REGULAR, dma((8,)), dma((3,)), dma((3,)), dma, dma((3,)), dma((3,)), dma((2,)), dma,
-            dma((3,)), dma((3,)), dma((3,)), dma((3,)), dma, dma, dma, dma,
+            pltpu.SemaphoreType.REGULAR, dma((9,)), dma((3,)), dma((3,)), dma, dma((3,)), dma((3,)), dma((2,)), dma,
+            dma((3,)), dma((12,)), dma((3,)), dma((3,)), dma, dma, dma, dma,
         ],
         compiler_params=pltpu.CompilerParams(
-            collective_id=0, has_side_effects=True, vmem_limit_bytes=63 * 1024 * 1024
+            collective_id=0, has_side_effects=True, vmem_limit_bytes=48 * 1024 * 1024
         ),
         name="triangle",
-    )(valid_count, pair_act, edge_proj, edge_gate, tri_gate, tri_out, attn_proj, bias_proj.T, attn_out).reshape(ROWS, COLS, CH)
+    )(valid_count.reshape(1, 1), *[pltpu.with_memory_space_constraint(a, pltpu.HBM) for a in (pair_act, edge_proj, edge_gate, tri_gate, tri_out, attn_proj, bias_proj.T, attn_out)]).reshape(ROWS, COLS, CH)
 
 
 def solution(mesh):

time: 60.8 us -> 59.3 us (0.975)
  local copies, waits for them, and re-layouts: 1.89 us -> 0.8 us
    unnamed x1, local copies, waits for them, and re-layouts: 1.89 us -> 0.8 us
where the time goes in v5:
time: 59.3 us; the launch traced here: 59.2 us
  Pallas kernels  57.7 us (97%)
  local copies, waits for them, and re-layouts  0.8 us (1%)
  between operations  0.66 us (1%)
    pallas_call x1, Pallas kernels, local(): pl.pallas_call(kernel, out_shape=jax.ShapeDtypeStruct((ROWS, 4, 2, 16, CH...  57.7 us

profile of v5, /device:TPU:1, one launch (start us, length us, event | category | flops | bytes accessed | tf_op | source)
XLA Modules:
  0.0 59.2 jit_solution(10937815981653982789)
XLA Ops:
  0.7 57.7 %triangle.1 = bf16[16,4,2,16,128]{4,3,2,1,0:T(8,128)(2,1)S(1)} custom-call(s32[1,1]{1,0:T(1,128)} %bitcast.3.count_in, bf16[16,128,128]{2,1,0:T(8,128)(2,1)} %pa_in.1, bf16[128,256]{1,0:T(8,128)(2,1)} %ep_in.1, bf16[128,256]{1,0:T(8,128)(2,1)} %eg_in.1, bf16[128,128]{1,0:T(8,128)(2,1)} %tg_in.1, bf16[128,128]{1,0:T(8,128)(2,1)} %to_in.1, ...), custom_call_target="tpu_custom_call" | custom-call | tf_op jit(solution)/shard_map/triangle/pallas_call | solution.py:462
  58.4 0.8 %copy.12 = bf16[16,128,128]{2,1,0:T(8,128)(2,1)} copy(bf16[16,128,128]{2,1,0:T(8,128)(2,1)S(1)} %bitcast.4) | data formatting | bytes 1048576

commit v6 on v5

--- a/solution.py
+++ b/solution.py
@@ -88,6 +88,14 @@
     def settle(ref, sem):
         pltpu.make_async_copy(ref, ref, sem).wait()
 
+    barrier = pltpu.get_barrier_semaphore()
+
+    plane = [o for o in OFFSETS if o[2] == 0 and o[3] == 0]
+    near = [o for o in OFFSETS if o[0] == 0 and o[1] == 0] + plane
+    for offset in near:
+        rr, qq = peer(offset)
+        pl.semaphore_signal(barrier, inc=1, device_id=(rr, qq), device_id_type=MESH)
+
     loads = [
         pltpu.make_async_copy(src, dst, load.at[n])
         for n, (src, dst) in enumerate(
@@ -96,14 +104,6 @@
     ]
     for copy in loads:
         copy.start()
-
-    barrier = pltpu.get_barrier_semaphore()
-
-    plane = [o for o in OFFSETS if o[2] == 0 and o[3] == 0]
-    near = [o for o in OFFSETS if o[0] == 0 and o[1] == 0] + plane
-    for offset in near:
-        rr, qq = peer(offset)
-        pl.semaphore_signal(barrier, inc=1, device_id=(rr, qq), device_id_type=MESH)
 
     for copy in loads:
         copy.wait()
@@ -231,6 +231,11 @@
                 tsend.at[half, own], trecv.at[me], t_send.at[half], t_recv, place(z, y, half), q
             ).start()
 
+    spot = lax.broadcasted_iota(jnp.int32, (16, HEADS), 0) % HEADS
+    pick = (spot == lax.broadcasted_iota(jnp.int32, (16, HEADS), 1)).astype(BF16)
+    bias_w = dot(pick, bp[...]).astype(BF16)
+    bias_row = lax.broadcasted_iota(jnp.int32, (16, 128), 0) // HEADS
+
     pa_local.wait()
     for copy in pa_copies:
         copy.wait()
@@ -243,15 +248,15 @@
     settle(trecv, t_recv)
 
     def add(part, total):
-        return total + jnp.sum(trecv[pl.ds(part * 16, 16)].astype(F32), axis=0)
-
-    mean = lax.fori_loop(0, 8, add, jnp.zeros((16, 128), F32)) * (1.0 / CH)
+        return total + jnp.sum(trecv[pl.ds(part * 32, 32)].astype(F32), axis=0)
+
+    mean = lax.fori_loop(0, 4, add, jnp.zeros((16, 128), F32)) * (1.0 / CH)
 
     def add_square(part, total):
-        centre = trecv[pl.ds(part * 16, 16)].astype(F32) - mean[None]
+        centre = trecv[pl.ds(part * 32, 32)].astype(F32) - mean[None]
         return total + jnp.sum(centre * centre, axis=0)
 
-    spread = lax.fori_loop(0, 8, add_square, jnp.zeros((16, 128), F32)) * (1.0 / CH)
+    spread = lax.fori_loop(0, 4, add_square, jnp.zeros((16, 128), F32)) * (1.0 / CH)
     gain = lax.rsqrt(spread + EPS)
 
     @pl.loop(0, 8)
@@ -259,11 +264,6 @@
         block = (trecv[pl.ds(part * 16, 16)].astype(F32) - mean[None]) * gain[None]
         for n in range(16):
             tn[pl.ds(part * 320 + n * 20, 16), :] = block[n]
-
-    spot = lax.broadcasted_iota(jnp.int32, (16, HEADS), 0) % HEADS
-    pick = (spot == lax.broadcasted_iota(jnp.int32, (16, HEADS), 1)).astype(BF16)
-    bias_w = dot(pick, bp[...]).astype(BF16)
-    bias_row = lax.broadcasted_iota(jnp.int32, (16, 128), 0) // HEADS
 
     u = z + core * (y - z)
     v = y + core * (z - y)

time: 59.3 us -> 59.3 us (level)
  no operation moved by 1% of the time
where the time goes in v6:
time: 59.3 us; the launch traced here: 59.2 us
  Pallas kernels  57.7 us (97%)
  local copies, waits for them, and re-layouts  0.8 us (1%)
  between operations  0.66 us (1%)
    pallas_call x1, Pallas kernels, local(): pl.pallas_call(kernel, out_shape=jax.ShapeDtypeStruct((ROWS, 4, 2, 16, CH...  57.7 us

profile of v6, /device:TPU:1, one launch (start us, length us, event | category | flops | bytes accessed | tf_op | source)
XLA Modules:
  0.0 59.2 jit_solution(5682180127285525469)
XLA Ops:
  0.7 57.7 %triangle.1 = bf16[16,4,2,16,128]{4,3,2,1,0:T(8,128)(2,1)S(1)} custom-call(s32[1,1]{1,0:T(1,128)} %bitcast.3.count_in, bf16[16,128,128]{2,1,0:T(8,128)(2,1)} %pa_in.1, bf16[128,256]{1,0:T(8,128)(2,1)} %ep_in.1, bf16[128,256]{1,0:T(8,128)(2,1)} %eg_in.1, bf16[128,128]{1,0:T(8,128)(2,1)} %tg_in.1, bf16[128,128]{1,0:T(8,128)(2,1)} %to_in.1, ...), custom_call_target="tpu_custom_call" | custom-call | tf_op jit(solution)/shard_map/triangle/pallas_call | solution.py:462
  58.4 0.8 %copy.12 = bf16[16,128,128]{2,1,0:T(8,128)(2,1)} copy(bf16[16,128,128]{2,1,0:T(8,128)(2,1)S(1)} %bitcast.4) | data formatting | bytes 1048576

commit v7 on v6

--- a/solution.py
+++ b/solution.py
@@ -420,18 +420,18 @@
         for d in (2, 1, 3):
             remote(osend.at[n, xs[d]], target, o_send, o_recv, place(z, y, owner), xs[d]).start()
 
+    @pl.loop(0, OWN)
+    def _(n):
+        attend(n, core)
+
+    target = out.at[pl.ds(q * OWN, OWN), :, core]
+    pltpu.make_async_copy(osend.at[0:OWN, q], target, o_recv).start()
+
     @pl.loop(OWN, 2 * OWN)
     def _(n):
         attend(n, 1 - core)
 
-    target = out.at[pl.ds(q * OWN, OWN), :, core]
     remote(osend.at[OWN : 2 * OWN, q], target, o_send, o_recv, twin, q).start()
-
-    @pl.loop(0, OWN)
-    def _(n):
-        attend(n, core)
-
-    pltpu.make_async_copy(osend.at[0:OWN, q], target, o_recv).start()
 
     settle(out, o_recv)
     settle(osend.at[0:7], o_send)

time: 59.3 us -> 59 us (level)
  no operation moved by 1% of the time
where the time goes in v7:
time: 59 us; the launch traced here: 58.8 us
  Pallas kernels  57.4 us (97%)
  local copies, waits for them, and re-layouts  0.8 us (1%)
  between operations  0.66 us (1%)
    pallas_call x1, Pallas kernels, local(): pl.pallas_call(kernel, out_shape=jax.ShapeDtypeStruct((ROWS, 4, 2, 16, CH...  57.4 us

profile of v7, /device:TPU:1, one launch (start us, length us, event | category | flops | bytes accessed | tf_op | source)
XLA Modules:
  0.0 58.8 jit_solution(2948317235679544112)
XLA Ops:
  0.7 57.4 %triangle.1 = bf16[16,4,2,16,128]{4,3,2,1,0:T(8,128)(2,1)S(1)} custom-call(s32[1,1]{1,0:T(1,128)} %bitcast.3.count_in, bf16[16,128,128]{2,1,0:T(8,128)(2,1)} %pa_in.1, bf16[128,256]{1,0:T(8,128)(2,1)} %ep_in.1, bf16[128,256]{1,0:T(8,128)(2,1)} %eg_in.1, bf16[128,128]{1,0:T(8,128)(2,1)} %tg_in.1, bf16[128,128]{1,0:T(8,128)(2,1)} %to_in.1, ...), custom_call_target="tpu_custom_call" | custom-call | tf_op jit(solution)/shard_map/triangle/pallas_call | solution.py:462
  58.0 0.8 %copy.12 = bf16[16,128,128]{2,1,0:T(8,128)(2,1)} copy(bf16[16,128,128]{2,1,0:T(8,128)(2,1)S(1)} %bitcast.4) | data formatting | bytes 1048576
